TPU v7x, 32 devices: a whole 2x2x4 slice. The times are simulated.
32 devices in a mesh: line: 8 (over y, x, core), seg: 4 (over z).
Axes of the slice: x: 2, y: 2, z: 4, core: 2. Of those that a mesh axis runs over, the one named last changes fastest.
Arguments:
- right_side: float32 [8, 32, 96, 128], P('line', 'seg'), may hold values from -24 to 24
- band_blocks: bfloat16 [8, 32, 4, 96, 96], P('line', 'seg')
- knot_pairs: int32 [8, 4, 6, 2, 2], P('line', 'seg'), may hold values from 0 to 7
- pair_counts: int32 [8, 4, 6], P('line', 'seg'), may hold values from 1 to 2, as said below
- cross_blocks: bfloat16 [8, 4, 6, 2, 96, 96], P('line', 'seg'), may hold values from -0.359375 to 0.359375
Outputs:
- solution: float32 [8, 32, 96, 128], P('line', 'seg')
Inputs may be any that keep to these rules, and one draw needn't show every extreme that they name: `knot_pairs`: entry s of bucket b counts only if s < pair_counts of that bucket; other entries are unused. `pair_counts`: every bucket holds at least one pair, and in every draw some line and segment has all buckets full.
All inputs are finite; a program needn't handle non-finite values.
Results may differ from a plain program's by a relative error of at most 0.0028.
Values may be sent and summed in bfloat16 or wider, within the bound.
A program may use at most 64 MiB of HBM per device.

v0:
```python
import jax
import jax.numpy as jnp
from jax import lax
from jax.sharding import PartitionSpec as P

ITERS = 3


LO_BOUND = 1.5
HI_BOUND = 12.0


def passed_along(value, axis, steps):
    count = lax.axis_size(axis)
    initial, last = (max(0, -steps), min(count, count - steps))
    return lax.ppermute(value, axis, [(source, source + steps) for source in range(initial, last)])


def passed_along_2(x, axis, by):
    count = lax.axis_size(axis)
    return lax.ppermute(x, axis, [(i, (i + by) % count) for i in range(count)])


def padded(block, sides, width):
    for axis, dim in sides:
        count = lax.axis_size(axis)
        forward = [(i, i + 1) for i in range(count - 1)]
        backward = [(target, source) for source, target in forward]
        low = lax.ppermute(
            lax.slice_in_dim(block, block.shape[dim] - width, None, axis=dim), axis, forward
        )
        high = lax.ppermute(lax.slice_in_dim(block, 0, width, axis=dim), axis, backward)
        block = jnp.concatenate([low, block, high], axis=dim)
    return block


def body(right_side, band_blocks, knot_pairs, pair_counts, cross_blocks):
    right_rows = right_side[0]
    blocks = band_blocks[0]
    my_pairs = knot_pairs[0, 0]
    used_count = pair_counts[0, 0]
    pair_coupling_term = cross_blocks[0, 0]
    count_of_knots = right_rows.shape[0]
    buckets = my_pairs.shape[0]
    slot_count = my_pairs.shape[1]
    group_span = buckets // 2 + 1
    offsets = [
        b - (group_span - 1) if b < group_span - 1 else b - group_span + 2 for b in range(buckets)
    ]
    boundary_blocks = passed_along(blocks[count_of_knots - 3 :], "seg", 1)
    lower_blocks = jnp.concatenate([boundary_blocks, blocks], axis=0)
    slot_ids = jnp.arange(slot_count, dtype=jnp.int32)
    asked_knots = []
    keep_masks = []
    for bucket, shift_by in enumerate(offsets):
        asked_knots.append(passed_along_2(my_pairs[bucket, :, 1], "line", shift_by))
        keep_masks.append((slot_ids < used_count[bucket]).astype(jnp.bfloat16)[:, None, None])
    center = (HI_BOUND + LO_BOUND) / 2.0
    radius = (HI_BOUND - LO_BOUND) / 2.0
    coeff = radius / center
    solution = jnp.zeros(right_rows.shape, jnp.float32)
    residual = right_rows
    direction = right_rows / center
    for turn in range(ITERS):
        probe_bf = direction.astype(jnp.bfloat16)
        solution = solution + direction
        extended = padded(probe_bf, (("seg", 0),), 3)
        summed = jnp.zeros(probe_bf.shape, jnp.float32)
        for step in range(4):
            summed = summed + jnp.einsum(
                "kab,kbr->kar",
                blocks[:, step],
                extended[3 + step : 3 + step + count_of_knots],
                preferred_element_type=jnp.float32,
            )
        for step in range(1, 4):
            summed = summed + jnp.einsum(
                "kba,kbr->kar",
                lower_blocks[3 - step : 3 - step + count_of_knots, step],
                extended[3 - step : 3 - step + count_of_knots],
                preferred_element_type=jnp.float32,
            )
        targets = []
        entry_values = []
        for apply_bucket, apply_shift_by in enumerate(offsets):
            answer_rows = jnp.take(probe_bf, asked_knots[apply_bucket], axis=0)
            fetched_rows = (
                passed_along_2(answer_rows, "line", -apply_shift_by) * keep_masks[apply_bucket]
            )
            entry_values.append(
                jnp.einsum(
                    "dqp,dpc->dqc",
                    pair_coupling_term[apply_bucket],
                    fetched_rows,
                    preferred_element_type=jnp.float32,
                )
            )
            targets.append(my_pairs[apply_bucket, :, 0])
            resident_rows = (
                jnp.take(probe_bf, my_pairs[apply_bucket, :, 0], axis=0) * keep_masks[apply_bucket]
            )
            product = jnp.einsum(
                "edu,edq->euq",
                pair_coupling_term[apply_bucket],
                resident_rows,
                preferred_element_type=jnp.float32,
            )
            entry_values.append(
                passed_along_2(product.astype(jnp.bfloat16), "line", apply_shift_by).astype(
                    product.dtype
                )
            )
            targets.append(asked_knots[apply_bucket])
        target_index = jnp.concatenate(targets, axis=0)
        target_values = jnp.concatenate(entry_values, axis=0)
        onehot = (
            jnp.arange(count_of_knots, dtype=jnp.int32)[:, None] == target_index[None, :]
        ).astype(jnp.float32)
        residual = residual - (
            summed
            + jnp.einsum("ks,spr->kpr", onehot, target_values, precision=lax.Precision.HIGHEST)
        )
        coeff_next = 1.0 / (2.0 * center / radius - coeff)
        direction = coeff_next * coeff * direction + 2.0 * coeff_next / radius * residual
        coeff = coeff_next
    return (solution + direction)[None]


def solution(mesh):
    return jax.shard_map(
        body,
        mesh=mesh,
        in_specs=(
            P("line", "seg", None, None),
            P("line", "seg", None, None, None),
            P("line", "seg", None, None, None),
            P("line", "seg", None),
            P("line", "seg", None, None, None, None),
        ),
        out_specs=P("line", "seg", None, None),
        check_vma=False,
    )
```

profile of v0, /device:TPU:1, one launch (start us, length us, event | category | flops | bytes accessed | tf_op | source)
XLA Modules:
  0.0 179.4 jit_solution(13823814008387691301)
XLA Ops:
  0.0 1.7 slice_reduce_fusion.1
  1.7 2.7 %collective-permute-start.8 = (s32[2]{0:T(128)S(1)}, s32[2]{0:T(128)S(1)}, u32[]{:S(2)}, u32[]{:S(2)}) collective-permute-start(s32[2]{0:T(128)S(1)} %get-tuple-element.7), channel_id=1, source_target_pairs={{0,12},{4,16},{8,20},{12,24},{16,28},{20,0},{24,4},{28,8},{1,13},{... | collective-permute-start | bytes 32 | tf_op jit(solution)/shard_map/ppermute | solution.py:21
  22.3 2.1 %collective-permute-start.3 = (s32[2]{0:T(128)S(1)}, s32[2]{0:T(128)S(1)}, u32[]{:S(2)}, u32[]{:S(2)}) collective-permute-start(s32[2]{0:T(128)S(1)} %get-tuple-element.16), channel_id=1, source_target_pairs={{0,20},{4,24},{8,28},{12,0},{16,4},{20,8},{24,12},{28,16},{1,21},{... | collective-permute-start | bytes 32 | tf_op jit(solution)/shard_map/ppermute | solution.py:21
  36.4 3.7 %collective-permute-done.11 = bf16[2,96,128]{2,1,0:T(8,128)(2,1)S(1)} collective-permute-done((bf16[2,96,128]{2,1,0:T(8,128)(2,1)S(1)}, bf16[2,96,128]{2,1,0:T(8,128)(2,1)S(1)}, u32[]{:S(2)}, u32[]{:S(2)}) %collective-permute-start.11) | collective-permute-done | bytes 49184 | tf_op jit(solution)/shard_map/ppermute | solution.py:21
  41.7 3.7 %collective-permute-start.15 = (bf16[2,96,128]{2,1,0:T(8,128)(2,1)S(1)}, bf16[2,96,128]{2,1,0:T(8,128)(2,1)S(1)}, u32[]{:S(2)}, u32[]{:S(2)}) collective-permute-start(bf16[2,96,128]{2,1,0:T(8,128)(2,1)S(1)} %broadcast_select_fusion.8), channel_id=1, source_target_pairs={{0,28},{4,0},{8,4},{12,8},{16,12},{20,16},{24,20},{28,24},{1,29},{... | collective-permute-start | bytes 147464 | tf_op jit(solution)/shard_map/ppermute | solution.py:21
  46.3 3.1 %collective-permute-start.17 = (bf16[2,96,128]{2,1,0:T(8,128)(2,1)S(1)}, bf16[2,96,128]{2,1,0:T(8,128)(2,1)S(1)}, u32[]{:S(2)}, u32[]{:S(2)}) collective-permute-start(bf16[2,96,128]{2,1,0:T(8,128)(2,1)S(1)} %broadcast_select_fusion.5), channel_id=1, source_target_pairs={{0,24},{4,28},{8,0},{12,4},{16,8},{20,12},{24,16},{28,20},{1,25},{... | collective-permute-start | bytes 147464 | tf_op jit(solution)/shard_map/ppermute | solution.py:21
  49.6 1.7 collective-permute-done.17
  58.6 4.0 %collective-permute-start.2 = (bf16[3,96,128]{2,1,0:T(8,128)(2,1)}, bf16[3,96,128]{2,1,0:T(8,128)(2,1)S(1)}, u32[]{:S(2)}, u32[]{:S(2)}) collective-permute-start(bf16[3,96,128]{2,1,0:T(8,128)(2,1)} %get-tuple-element.28), channel_id=1, source_target_pairs={{0,1},{1,2},{2,3},{4,5},{5,6},{6,7},{8,9},{9,10},{10,11},{12,13},{... | collective-permute-start | bytes 221192 | tf_op jit(solution)/shard_map/ppermute | solution.py:29
  62.6 4.0 %collective-permute-start.1 = (bf16[3,4,96,96]{3,2,0,1:T(8,128)(2,1)}, bf16[3,4,96,96]{3,2,0,1:T(8,128)(2,1)}, u32[]{:S(2)}, u32[]{:S(2)}) collective-permute-start(bf16[3,4,96,96]{3,2,0,1:T(8,128)(2,1)} %slice_bitcast_fusion), channel_id=1, source_target_pairs={{0,1},{1,2},{2,3},{4,5},{5,6},{6,7},{8,9},{9,10},{10,11},{12,13},{... | collective-permute-start | bytes 663560 | tf_op jit(solution)/shard_map/ppermute | solution.py:16
  67.2 3.3 %concatenate.54 = f32[24,96,128]{2,0,1:T(8,128)S(1)} concatenate(f32[2,96,128]{2,0,1:T(2,128)S(1)} %bitcast.322, bf16[2,96,128]{2,0,1:T(2,128)(2,1)} %copy-done.13, f32[2,96,128]{2,0,1:T(2,128)S(1)} %bitcast.323, bf16[2,96,128]{2,0,1:T(2,128)(2,1)} %copy-done.14, f32[2,96,128]{2,0,1:T(2,128)S(1)} %bitcast.324, bf16[2,96,128]{2,0,1:T(2,128)(2,1)} %copy-done.15, ...), dimensions={0} | concatenate | bytes 2064384 | tf_op jit(solution)/shard_map/concatenate | solution.py:115
  85.6 2.4 %collective-permute-start.23 = (bf16[2,96,128]{2,1,0:T(8,128)(2,1)S(1)}, bf16[2,96,128]{2,1,0:T(8,128)(2,1)S(1)}, u32[]{:S(2)}, u32[]{:S(2)}) collective-permute-start(bf16[2,96,128]{2,1,0:T(8,128)(2,1)S(1)} %broadcast_select_fusion.16), channel_id=1, source_target_pairs={{0,12},{4,16},{8,20},{12,24},{16,28},{20,0},{24,4},{28,8},{1,13},{... | collective-permute-start | bytes 147464 | tf_op jit(solution)/shard_map/ppermute | solution.py:21
  89.3 2.0 %collective-permute-start.26 = (bf16[2,96,128]{2,0,1:T(2,128)(2,1)S(1)}, bf16[2,96,128]{2,0,1:T(2,128)(2,1)S(1)}, u32[]{:S(2)}, u32[]{:S(2)}) collective-permute-start(bf16[2,96,128]{2,0,1:T(2,128)(2,1)S(1)} %bitcast.356), channel_id=1, source_target_pairs={{0,24},{4,28},{8,0},{12,4},{16,8},{20,12},{24,16},{28,20},{1,25},{... | collective-permute-start | bytes 147464 | tf_op jit(solution)/shard_map/ppermute | solution.py:21
  92.8 2.7 %collective-permute-start.29 = (bf16[2,96,128]{2,1,0:T(8,128)(2,1)S(1)}, bf16[2,96,128]{2,1,0:T(8,128)(2,1)S(1)}, u32[]{:S(2)}, u32[]{:S(2)}) collective-permute-start(bf16[2,96,128]{2,1,0:T(8,128)(2,1)S(1)} %broadcast_select_fusion.7), channel_id=1, source_target_pairs={{0,28},{4,0},{8,4},{12,8},{16,12},{20,16},{24,20},{28,24},{1,29},{... | collective-permute-start | bytes 147464 | tf_op jit(solution)/shard_map/ppermute | solution.py:21
  96.9 3.4 %collective-permute-start.31 = (bf16[2,96,128]{2,1,0:T(8,128)(2,1)S(1)}, bf16[2,96,128]{2,1,0:T(8,128)(2,1)S(1)}, u32[]{:S(2)}, u32[]{:S(2)}) collective-permute-start(bf16[2,96,128]{2,1,0:T(8,128)(2,1)S(1)} %broadcast_select_fusion.4), channel_id=1, source_target_pairs={{0,24},{4,28},{8,0},{12,4},{16,8},{20,12},{24,16},{28,20},{1,25},{... | collective-permute-start | bytes 147464 | tf_op jit(solution)/shard_map/ppermute | solution.py:21
  112.3 4.9 %collective-permute-start.22 = (bf16[3,96,128]{2,1,0:T(8,128)(2,1)}, bf16[3,96,128]{2,1,0:T(8,128)(2,1)S(1)}, u32[]{:S(2)}, u32[]{:S(2)}) collective-permute-start(bf16[3,96,128]{2,1,0:T(8,128)(2,1)} %get-tuple-element.26), channel_id=1, source_target_pairs={{0,1},{1,2},{2,3},{4,5},{5,6},{6,7},{8,9},{9,10},{10,11},{12,13},{... | collective-permute-start | bytes 221192 | tf_op jit(solution)/shard_map/ppermute | solution.py:29
  117.9 3.5 %concatenate.57 = f32[24,96,128]{2,0,1:T(8,128)S(1)} concatenate(f32[2,96,128]{2,0,1:T(2,128)} %bitcast.327, bf16[2,96,128]{2,0,1:T(2,128)(2,1)} %copy-done.18, f32[2,96,128]{2,0,1:T(2,128)} %bitcast.330, bf16[2,96,128]{2,0,1:T(2,128)(2,1)} %copy-done.20, f32[2,96,128]{2,0,1:T(2,128)} %bitcast.332, bf16[2,96,128]{2,0,1:T(2,128)(2,1)} %copy-done.22, f32[2,96,128]{2,0,1:T(2,128)} %bitcast.334, ...), dimensions={0} | concatenate | bytes 2064384 | tf_op jit(solution)/shard_map/concatenate | solution.py:115
  123.8 1.9 %fusion.27 = (bf16[8,96,128]{2,1,0:T(8,128)(2,1)S(1)}, f32[8,96,128]{2,1,0:T(8,128)}) fusion(f32[8,96,128]{2,1,0:T(8,128)S(1)} %get-tuple-element.36, f32[1,8,96,128]{3,2,1,0:T(8,128)S(1)} %copy-done, f32[8,96,128]{2,0,1:T(8,128)S(1)} %fusion.258, f32[8,96,128]{2,1,0:T(8,128)S(1)} %fusion.62, f32[8,96,128]{2,1,0:T(8,128)S(1)} %fusion.39, ...), kind=kOutput, calls=%fused_computation.102 | convolution fusion | flops 20643840 | bytes 4202496 | tf_op jit(solution)/shard_map/kab,kbr->kar/dot_general | solution.py:70
  137.4 1.8 %collective-permute-start.37 = (bf16[2,96,128]{2,1,0:T(8,128)(2,1)S(1)}, bf16[2,96,128]{2,1,0:T(8,128)(2,1)S(1)}, u32[]{:S(2)}, u32[]{:S(2)}) collective-permute-start(bf16[2,96,128]{2,1,0:T(8,128)(2,1)S(1)} %broadcast_select_fusion.15), channel_id=1, source_target_pairs={{0,12},{4,16},{8,20},{12,24},{16,28},{20,0},{24,4},{28,8},{1,13},{... | collective-permute-start | bytes 147464 | tf_op jit(solution)/shard_map/ppermute | solution.py:21
  140.5 2.3 %collective-permute-start.40 = (bf16[2,96,128]{2,0,1:T(2,128)(2,1)S(1)}, bf16[2,96,128]{2,0,1:T(2,128)(2,1)S(1)}, u32[]{:S(2)}, u32[]{:S(2)}) collective-permute-start(bf16[2,96,128]{2,0,1:T(2,128)(2,1)S(1)} %bitcast.355), channel_id=1, source_target_pairs={{0,24},{4,28},{8,0},{12,4},{16,8},{20,12},{24,16},{28,20},{1,25},{... | collective-permute-start | bytes 147464 | tf_op jit(solution)/shard_map/ppermute | solution.py:21
  144.3 2.4 %collective-permute-start.43 = (bf16[2,96,128]{2,1,0:T(8,128)(2,1)S(1)}, bf16[2,96,128]{2,1,0:T(8,128)(2,1)S(1)}, u32[]{:S(2)}, u32[]{:S(2)}) collective-permute-start(bf16[2,96,128]{2,1,0:T(8,128)(2,1)S(1)} %broadcast_select_fusion.6), channel_id=1, source_target_pairs={{0,28},{4,0},{8,4},{12,8},{16,12},{20,16},{24,20},{28,24},{1,29},{... | collective-permute-start | bytes 147464 | tf_op jit(solution)/shard_map/ppermute | solution.py:21
  147.8 3.7 %collective-permute-start.45 = (bf16[2,96,128]{2,1,0:T(8,128)(2,1)S(1)}, bf16[2,96,128]{2,1,0:T(8,128)(2,1)S(1)}, u32[]{:S(2)}, u32[]{:S(2)}) collective-permute-start(bf16[2,96,128]{2,1,0:T(8,128)(2,1)S(1)} %broadcast_select_fusion.3), channel_id=1, source_target_pairs={{0,24},{4,28},{8,0},{12,4},{16,8},{20,12},{24,16},{28,20},{1,25},{... | collective-permute-start | bytes 147464 | tf_op jit(solution)/shard_map/ppermute | solution.py:21
  162.2 4.9 %collective-permute-start.36 = (bf16[3,96,128]{2,1,0:T(8,128)(2,1)}, bf16[3,96,128]{2,1,0:T(8,128)(2,1)}, u32[]{:S(2)}, u32[]{:S(2)}) collective-permute-start(bf16[3,96,128]{2,1,0:T(8,128)(2,1)} %get-tuple-element.24), channel_id=1, source_target_pairs={{0,1},{1,2},{2,3},{4,5},{5,6},{6,7},{8,9},{9,10},{10,11},{12,13},{... | collective-permute-start | bytes 221192 | tf_op jit(solution)/shard_map/ppermute | solution.py:29
  167.8 3.4 %concatenate.60 = f32[24,96,128]{2,0,1:T(8,128)S(1)} concatenate(f32[2,96,128]{2,0,1:T(2,128)S(1)} %bitcast.328, bf16[2,96,128]{2,0,1:T(2,128)(2,1)} %copy-done.17, f32[2,96,128]{2,0,1:T(2,128)S(1)} %bitcast.331, bf16[2,96,128]{2,0,1:T(2,128)(2,1)} %copy-done.19, f32[2,96,128]{2,0,1:T(2,128)} %bitcast.333, bf16[2,96,128]{2,0,1:T(2,128)(2,1)} %copy-done.21, ...), dimensions={0} | concatenate | bytes 2064384 | tf_op jit(solution)/shard_map/concatenate | solution.py:115
  177.5 1.9 %fusion.24 = f32[1,8,96,128]{3,2,1,0:T(8,128)} fusion(f32[8,96,128]{2,1,0:T(8,128)S(1)} %copy-done.6, f32[8,96,128]{2,1,0:T(8,128)S(1)} %fusion.58, f32[8,96,128]{2,1,0:T(8,128)S(1)} %fusion.29, f32[8,96,128]{2,1,0:T(8,128)S(1)} %fusion.32, f32[8,128,96]{1,2,0:T(8,128)S(1)} %fusion.60, f32[8,128,96]{1,2,0:T(8,128)S(1)} %convolution_add_fusion.1, ...), kind=kOutput, calls=%fused_computation.66 | convolution fusion | flops 21233664 | bytes 4399104 | tf_op jit(solution)/shard_map/kab,kbr->kar/dot_general | solution.py:70
  (469 shorter events, 105.8 us)
Async XLA Ops:
  1.7 20.6 %collective-permute-start.8 = (s32[2]{0:T(128)S(1)}, s32[2]{0:T(128)S(1)}, u32[]{:S(2)}, u32[]{:S(2)}) collective-permute-start(s32[2]{0:T(128)S(1)} %get-tuple-element.7), channel_id=1, source_target_pairs={{0,12},{4,16},{8,20},{12,24},{16,28},{20,0},{24,4},{28,8},{1,13},{... | collective-permute-start | bytes 32 | tf_op jit(solution)/shard_map/ppermute | solution.py:21
  4.4 20.1 %collective-permute-start.7 = (s32[2]{0:T(128)S(1)}, s32[2]{0:T(128)S(1)}, u32[]{:S(2)}, u32[]{:S(2)}) collective-permute-start(s32[2]{0:T(128)S(1)} %get-tuple-element.8), channel_id=1, source_target_pairs={{0,8},{4,12},{8,16},{12,20},{16,24},{20,28},{24,0},{28,4},{1,9},{5... | collective-permute-start | bytes 32 | tf_op jit(solution)/shard_map/ppermute | solution.py:21
  5.6 19.0 %collective-permute-start.6 = (s32[2]{0:T(128)S(1)}, s32[2]{0:T(128)S(1)}, u32[]{:S(2)}, u32[]{:S(2)}) collective-permute-start(s32[2]{0:T(128)S(1)} %get-tuple-element.10), channel_id=1, source_target_pairs={{0,4},{4,8},{8,12},{12,16},{16,20},{20,24},{24,28},{28,0},{1,5},{5... | collective-permute-start | bytes 32 | tf_op jit(solution)/shard_map/ppermute | solution.py:21
  6.8 19.0 %collective-permute-start.5 = (s32[2]{0:T(128)S(1)}, s32[2]{0:T(128)S(1)}, u32[]{:S(2)}, u32[]{:S(2)}) collective-permute-start(s32[2]{0:T(128)S(1)} %get-tuple-element.12), channel_id=1, source_target_pairs={{0,28},{4,0},{8,4},{12,8},{16,12},{20,16},{24,20},{28,24},{1,29},{... | collective-permute-start | bytes 32 | tf_op jit(solution)/shard_map/ppermute | solution.py:21
  6.8 20.0 %collective-permute-start.4 = (s32[2]{0:T(128)S(1)}, s32[2]{0:T(128)S(1)}, u32[]{:S(2)}, u32[]{:S(2)}) collective-permute-start(s32[2]{0:T(128)S(1)} %get-tuple-element.14), channel_id=1, source_target_pairs={{0,24},{4,28},{8,0},{12,4},{16,8},{20,12},{24,16},{28,20},{1,25},{... | collective-permute-start | bytes 32 | tf_op jit(solution)/shard_map/ppermute | solution.py:21
  24.5 27.5 %collective-permute-start.10 = (bf16[2,96,128]{2,0,1:T(2,128)(2,1)S(1)}, bf16[2,96,128]{2,0,1:T(2,128)(2,1)S(1)}, u32[]{:S(2)}, u32[]{:S(2)}) collective-permute-start(bf16[2,96,128]{2,0,1:T(2,128)(2,1)S(1)} %bitcast.346), channel_id=1, source_target_pairs={{0,20},{4,24},{8,28},{12,0},{16,4},{20,8},{24,12},{28,16},{1,21},{... | collective-permute-start | bytes 147464 | tf_op jit(solution)/shard_map/ppermute | solution.py:21
  24.6 32.7 %collective-permute-start.12 = (bf16[2,96,128]{2,0,1:T(2,128)(2,1)S(1)}, bf16[2,96,128]{2,0,1:T(2,128)(2,1)S(1)}, u32[]{:S(2)}, u32[]{:S(2)}) collective-permute-start(bf16[2,96,128]{2,0,1:T(2,128)(2,1)S(1)} %bitcast.345), channel_id=1, source_target_pairs={{0,24},{4,28},{8,0},{12,4},{16,8},{20,12},{24,16},{28,20},{1,25},{... | collective-permute-start | bytes 147464 | tf_op jit(solution)/shard_map/ppermute | solution.py:21
  25.8 32.8 %collective-permute-start.14 = (bf16[2,96,128]{2,0,1:T(2,128)(2,1)S(1)}, bf16[2,96,128]{2,0,1:T(2,128)(2,1)S(1)}, u32[]{:S(2)}, u32[]{:S(2)}) collective-permute-start(bf16[2,96,128]{2,0,1:T(2,128)(2,1)S(1)} %bitcast.344), channel_id=1, source_target_pairs={{0,28},{4,0},{8,4},{12,8},{16,12},{20,16},{24,20},{28,24},{1,29},{... | collective-permute-start | bytes 147464 | tf_op jit(solution)/shard_map/ppermute | solution.py:21
  26.8 35.8 %collective-permute-start.16 = (bf16[2,96,128]{2,0,1:T(2,128)(2,1)S(1)}, bf16[2,96,128]{2,0,1:T(2,128)(2,1)S(1)}, u32[]{:S(2)}, u32[]{:S(2)}) collective-permute-start(bf16[2,96,128]{2,0,1:T(2,128)(2,1)S(1)} %bitcast.343), channel_id=1, source_target_pairs={{0,4},{4,8},{8,12},{12,16},{16,20},{20,24},{24,28},{28,0},{1,5},{5... | collective-permute-start | bytes 147464 | tf_op jit(solution)/shard_map/ppermute | solution.py:21
  52.0 14.6 %collective-permute-start.18 = (bf16[2,96,128]{2,0,1:T(2,128)(2,1)S(1)}, bf16[2,96,128]{2,0,1:T(2,128)(2,1)S(1)}, u32[]{:S(2)}, u32[]{:S(2)}) collective-permute-start(bf16[2,96,128]{2,0,1:T(2,128)(2,1)S(1)} %bitcast.342), channel_id=1, source_target_pairs={{0,8},{4,12},{8,16},{12,20},{16,24},{20,28},{24,0},{28,4},{1,9},{5... | collective-permute-start | bytes 147464 | tf_op jit(solution)/shard_map/ppermute | solution.py:21
  57.3 13.7 %collective-permute-start = (bf16[3,96,128]{2,1,0:T(8,128)(2,1)}, bf16[3,96,128]{2,1,0:T(8,128)(2,1)S(1)}, u32[]{:S(2)}, u32[]{:S(2)}) collective-permute-start(bf16[3,96,128]{2,1,0:T(8,128)(2,1)} %get-tuple-element.27), channel_id=1, source_target_pairs={{1,0},{2,1},{3,2},{5,4},{6,5},{7,6},{9,8},{10,9},{11,10},{13,12},{... | collective-permute-start | bytes 221192 | tf_op jit(solution)/shard_map/ppermute | solution.py:32
  58.6 14.1 %collective-permute-start.2 = (bf16[3,96,128]{2,1,0:T(8,128)(2,1)}, bf16[3,96,128]{2,1,0:T(8,128)(2,1)S(1)}, u32[]{:S(2)}, u32[]{:S(2)}) collective-permute-start(bf16[3,96,128]{2,1,0:T(8,128)(2,1)} %get-tuple-element.28), channel_id=1, source_target_pairs={{0,1},{1,2},{2,3},{4,5},{5,6},{6,7},{8,9},{9,10},{10,11},{12,13},{... | collective-permute-start | bytes 221192 | tf_op jit(solution)/shard_map/ppermute | solution.py:29
  88.4 14.3 %collective-permute-start.24 = (bf16[2,96,128]{2,0,1:T(2,128)(2,1)S(1)}, bf16[2,96,128]{2,0,1:T(2,128)(2,1)S(1)}, u32[]{:S(2)}, u32[]{:S(2)}) collective-permute-start(bf16[2,96,128]{2,0,1:T(2,128)(2,1)S(1)} %bitcast.358), channel_id=1, source_target_pairs={{0,20},{4,24},{8,28},{12,0},{16,4},{20,8},{24,12},{28,16},{1,21},{... | collective-permute-start | bytes 147464 | tf_op jit(solution)/shard_map/ppermute | solution.py:21
  89.3 21.7 %collective-permute-start.26 = (bf16[2,96,128]{2,0,1:T(2,128)(2,1)S(1)}, bf16[2,96,128]{2,0,1:T(2,128)(2,1)S(1)}, u32[]{:S(2)}, u32[]{:S(2)}) collective-permute-start(bf16[2,96,128]{2,0,1:T(2,128)(2,1)S(1)} %bitcast.356), channel_id=1, source_target_pairs={{0,24},{4,28},{8,0},{12,4},{16,8},{20,12},{24,16},{28,20},{1,25},{... | collective-permute-start | bytes 147464 | tf_op jit(solution)/shard_map/ppermute | solution.py:21
  92.1 20.2 %collective-permute-start.28 = (bf16[2,96,128]{2,0,1:T(2,128)(2,1)S(1)}, bf16[2,96,128]{2,0,1:T(2,128)(2,1)S(1)}, u32[]{:S(2)}, u32[]{:S(2)}) collective-permute-start(bf16[2,96,128]{2,0,1:T(2,128)(2,1)S(1)} %bitcast.354), channel_id=1, source_target_pairs={{0,28},{4,0},{8,4},{12,8},{16,12},{20,16},{24,20},{28,24},{1,29},{... | collective-permute-start | bytes 147464 | tf_op jit(solution)/shard_map/ppermute | solution.py:21
  95.7 21.5 %collective-permute-start.30 = (bf16[2,96,128]{2,0,1:T(2,128)(2,1)S(1)}, bf16[2,96,128]{2,0,1:T(2,128)(2,1)S(1)}, u32[]{:S(2)}, u32[]{:S(2)}) collective-permute-start(bf16[2,96,128]{2,0,1:T(2,128)(2,1)S(1)} %bitcast.352), channel_id=1, source_target_pairs={{0,4},{4,8},{8,12},{12,16},{16,20},{20,24},{24,28},{28,0},{1,5},{5... | collective-permute-start | bytes 147464 | tf_op jit(solution)/shard_map/ppermute | solution.py:21
  102.7 14.5 %collective-permute-start.32 = (bf16[2,96,128]{2,0,1:T(2,128)(2,1)S(1)}, bf16[2,96,128]{2,0,1:T(2,128)(2,1)S(1)}, u32[]{:S(2)}, u32[]{:S(2)}) collective-permute-start(bf16[2,96,128]{2,0,1:T(2,128)(2,1)S(1)} %bitcast.350), channel_id=1, source_target_pairs={{0,8},{4,12},{8,16},{12,20},{16,24},{20,28},{24,0},{28,4},{1,9},{5... | collective-permute-start | bytes 147464 | tf_op jit(solution)/shard_map/ppermute | solution.py:21
  111.0 12.2 %collective-permute-start.21 = (bf16[3,96,128]{2,1,0:T(8,128)(2,1)}, bf16[3,96,128]{2,1,0:T(8,128)(2,1)S(1)}, u32[]{:S(2)}, u32[]{:S(2)}) collective-permute-start(bf16[3,96,128]{2,1,0:T(8,128)(2,1)} %get-tuple-element.25), channel_id=1, source_target_pairs={{1,0},{2,1},{3,2},{5,4},{6,5},{7,6},{9,8},{10,9},{11,10},{13,12},{... | collective-permute-start | bytes 221192 | tf_op jit(solution)/shard_map/ppermute | solution.py:32
  139.6 14.3 %collective-permute-start.38 = (bf16[2,96,128]{2,0,1:T(2,128)(2,1)S(1)}, bf16[2,96,128]{2,0,1:T(2,128)(2,1)S(1)}, u32[]{:S(2)}, u32[]{:S(2)}) collective-permute-start(bf16[2,96,128]{2,0,1:T(2,128)(2,1)S(1)} %bitcast.357), channel_id=1, source_target_pairs={{0,20},{4,24},{8,28},{12,0},{16,4},{20,8},{24,12},{28,16},{1,21},{... | collective-permute-start | bytes 147464 | tf_op jit(solution)/shard_map/ppermute | solution.py:21
  140.5 20.4 %collective-permute-start.40 = (bf16[2,96,128]{2,0,1:T(2,128)(2,1)S(1)}, bf16[2,96,128]{2,0,1:T(2,128)(2,1)S(1)}, u32[]{:S(2)}, u32[]{:S(2)}) collective-permute-start(bf16[2,96,128]{2,0,1:T(2,128)(2,1)S(1)} %bitcast.355), channel_id=1, source_target_pairs={{0,24},{4,28},{8,0},{12,4},{16,8},{20,12},{24,16},{28,20},{1,25},{... | collective-permute-start | bytes 147464 | tf_op jit(solution)/shard_map/ppermute | solution.py:21
  143.1 19.1 %collective-permute-start.42 = (bf16[2,96,128]{2,0,1:T(2,128)(2,1)S(1)}, bf16[2,96,128]{2,0,1:T(2,128)(2,1)S(1)}, u32[]{:S(2)}, u32[]{:S(2)}) collective-permute-start(bf16[2,96,128]{2,0,1:T(2,128)(2,1)S(1)} %bitcast.353), channel_id=1, source_target_pairs={{0,28},{4,0},{8,4},{12,8},{16,12},{20,16},{24,20},{28,24},{1,29},{... | collective-permute-start | bytes 147464 | tf_op jit(solution)/shard_map/ppermute | solution.py:21
  146.9 20.2 %collective-permute-start.44 = (bf16[2,96,128]{2,0,1:T(2,128)(2,1)S(1)}, bf16[2,96,128]{2,0,1:T(2,128)(2,1)S(1)}, u32[]{:S(2)}, u32[]{:S(2)}) collective-permute-start(bf16[2,96,128]{2,0,1:T(2,128)(2,1)S(1)} %bitcast.351), channel_id=1, source_target_pairs={{0,4},{4,8},{8,12},{12,16},{16,20},{20,24},{24,28},{28,0},{1,5},{5... | collective-permute-start | bytes 147464 | tf_op jit(solution)/shard_map/ppermute | solution.py:21
  153.9 13.2 %collective-permute-start.46 = (bf16[2,96,128]{2,0,1:T(2,128)(2,1)S(1)}, bf16[2,96,128]{2,0,1:T(2,128)(2,1)S(1)}, u32[]{:S(2)}, u32[]{:S(2)}) collective-permute-start(bf16[2,96,128]{2,0,1:T(2,128)(2,1)S(1)} %bitcast.349), channel_id=1, source_target_pairs={{0,8},{4,12},{8,16},{12,20},{16,24},{20,28},{24,0},{28,4},{1,9},{5... | collective-permute-start | bytes 147464 | tf_op jit(solution)/shard_map/ppermute | solution.py:21
  160.9 14.5 %collective-permute-start.35 = (bf16[3,96,128]{2,1,0:T(8,128)(2,1)}, bf16[3,96,128]{2,1,0:T(8,128)(2,1)}, u32[]{:S(2)}, u32[]{:S(2)}) collective-permute-start(bf16[3,96,128]{2,1,0:T(8,128)(2,1)} %get-tuple-element.23), channel_id=1, source_target_pairs={{1,0},{2,1},{3,2},{5,4},{6,5},{7,6},{9,8},{10,9},{11,10},{13,12},{... | collective-permute-start | bytes 221192 | tf_op jit(solution)/shard_map/ppermute | solution.py:32
  (123 other events, 1083.0 us)
where the time goes:
time: 182 us; the launch traced here: 179 us
  starting transfers between devices  74.3 us (41%)
  local copies, waits for them, and re-layouts  53.9 us (30%)
  matrix products  23.7 us (13%)
  waiting for transfers between devices  17.8 us (10%)
  other arithmetic  7.42 us (4%)
  between operations  2.32 us (1%)
    ppermute x42, starting transfers between devices, passed_along_2(): return lax.ppermute(x, axis, [(i, (i + by) % count) for i in range(count)])  52.7 us
    ppermute x42, waiting for transfers between devices, passed_along_2(): return lax.ppermute(x, axis, [(i, (i + by) % count) for i in range(count)])  17.8 us
    ppermute x3, starting transfers between devices, padded(): lax.ppermute(lax.slice_in_dim(block, block.shape[dim] - width, None, axis...  13.8 us
    gather x18, local copies, waits for them, and re-layouts, body(): answer_rows = jnp.take(probe_bf, asked_knots[apply_bucket], axis=0)  11.6 us
    gather x18, local copies, waits for them, and re-layouts, body(): jnp.take(probe_bf, my_pairs[apply_bucket, :, 0], axis=0)  11 us
    concatenate x3, local copies, waits for them, and re-layouts, body(): target_values = jnp.concatenate(entry_values, axis=0)  10.2 us
    dot_general x12, matrix products, body(): jnp.einsum('kab,kbr->kar', blocks[:, step], extended[3 + step:3 + step +...  9.07 us
    dot_general x18, local copies, waits for them, and re-layouts, body(): jnp.einsum('dqp,dpc->dqc', pair_coupling_term[apply_bucket], fetched_rows...  8.35 us
  transfers between devices with their start and end apart: 49, of which 13 were waited for; matrix products, arithmetic and copies ran while one was open for 27% of the time, Pallas kernels for 0%

commit v1 on v0

v1 whole, which is shorter than its diff:
```python
import functools

import jax
import jax.numpy as jnp
from jax import lax
from jax.experimental import pallas as pl
from jax.experimental.pallas import tpu as pltpu
from jax.sharding import PartitionSpec as P

ITERS = 3
HALO = 3
LO_BOUND = 1.5
HI_BOUND = 12.0
MESH = pl.DeviceIdType.MESH


def kernel(lines, segs, offsets, slots, *refs):
    (meta_ref, meta_vec, rhs, band, cross, out) = refs[:6]
    (wide, cmask, ctrans, lower, meta_in, meta_far, resid, direc) = refs[6:14]
    per = [refs[14 + 6 * t : 20 + 6 * t] for t in range(ITERS)]
    send_sem, recv_sem, local_sem = refs[14 + 6 * ITERS :]
    knots, params, probes = rhs.shape
    buckets = len(offsets)
    line = lax.axis_index("line")
    seg = lax.axis_index("seg")
    has_prev = seg > 0
    has_next = seg < segs - 1

    def line_at(shift):
        return (lax.rem(line + (shift + lines), lines), seg)

    prev_dev = (line, jnp.maximum(seg - 1, 0))
    next_dev = (line, jnp.minimum(seg + 1, segs - 1))

    barrier = pltpu.get_barrier_semaphore()
    for off in offsets:
        pl.semaphore_signal(barrier, inc=1, device_id=line_at(off), device_id_type=MESH)

    @pl.when(has_prev)
    def _():
        pl.semaphore_signal(barrier, inc=1, device_id=prev_dev, device_id_type=MESH)

    @pl.when(has_next)
    def _():
        pl.semaphore_signal(barrier, inc=1, device_id=next_dev, device_id_type=MESH)

    center = (HI_BOUND + LO_BOUND) / 2.0
    radius = (HI_BOUND - LO_BOUND) / 2.0
    coeff = radius / center

    for k in range(knots):
        first = rhs[k] / center
        direc[k] = first
        resid[k] = rhs[k]
        out[k] = first
        per[0][0][k] = first.astype(jnp.bfloat16)

    pl.semaphore_wait(
        barrier, buckets + has_prev.astype(jnp.int32) + has_next.astype(jnp.int32)
    )

    def remote(src, dst, sem, device):
        return pltpu.make_async_remote_copy(
            src_ref=src,
            dst_ref=dst,
            send_sem=send_sem.at[sem],
            recv_sem=recv_sem.at[sem],
            device_id=device,
            device_id_type=MESH,
        )

    meta_copies = [
        remote(meta_vec, meta_in.at[b], b, line_at(off)) for b, off in enumerate(offsets)
    ]
    for copy in meta_copies:
        copy.start()
    lower_copy = remote(band.at[pl.ds(knots - HALO, HALO)], lower, buckets, next_dev)
    base = buckets + 1
    stride = 2 * buckets + 2

    def halo_copies(t):
        own, ext = per[t][0], per[t][1]
        at = base + t * stride
        up = remote(own.at[pl.ds(knots - HALO, HALO)], ext.at[pl.ds(0, HALO)], at, next_dev)
        down = remote(own.at[pl.ds(0, HALO)], ext.at[pl.ds(HALO + knots, HALO)], at + 1, prev_dev)
        return up, down

    def start_halos(t):
        up, down = halo_copies(t)

        @pl.when(has_next)
        def _():
            up.start()

        @pl.when(has_prev)
        def _():
            down.start()

    start_halos(0)

    @pl.when(has_next)
    def _():
        lower_copy.start()

    def own_index(b, s, which):
        return meta_ref[0, (b * slots + s) * 2 + which]

    def far_index(b, s):
        return meta_far[b, 0, (b * slots + s) * 2 + 1]

    for b in range(buckets):
        for s in range(slots):
            keep = (s < meta_ref[0, buckets * slots * 2 + b]).astype(jnp.float32)
            block = cross[b * slots + s].astype(jnp.float32) * keep
            cmask[b * slots + s] = block.astype(jnp.bfloat16)
            ctrans[b * slots + s] = block.T.astype(jnp.bfloat16)

    for copy in meta_copies:
        copy.wait_recv()
    to_scalar = pltpu.make_async_copy(meta_in, meta_far, local_sem)
    to_scalar.start()
    to_scalar.wait()

    def start_partners(t):
        own, _, sent_v, sent_p, got_v, got_p = per[t]
        at = base + t * stride + 2
        copies_v, copies_p = [], []
        for b, off in enumerate(offsets):
            for s in range(slots):
                sent_v[b, s] = own[far_index(b, s)]
            copy = remote(sent_v.at[b], got_v.at[b], at + b, line_at(-off))
            copy.start()
            copies_v.append(copy)
        for b, off in enumerate(offsets):
            for s in range(slots):
                sent_p[b, s] = jnp.dot(
                    ctrans[b * slots + s],
                    own[own_index(b, s, 0)],
                    preferred_element_type=jnp.float32,
                ).astype(jnp.bfloat16)
            copy = remote(sent_p.at[b], got_p.at[b], at + buckets + b, line_at(off))
            copy.start()
            copies_p.append(copy)
        return copies_v, copies_p

    partner_copies = start_partners(0)

    @pl.when(has_prev)
    def _():
        lower_copy.wait_recv()

    @pl.when(jnp.logical_not(has_prev))
    def _():
        lower[...] = jnp.zeros_like(lower)

    for k in range(knots):
        for step in range(HALO + 1):
            at = (HALO + step) * params
            wide[k, :, at : at + params] = band[k, step]
        for step in range(1, HALO + 1):
            at = (HALO - step) * params
            source = band[k - step, step] if k >= step else lower[HALO + k - step, step]
            wide[k, :, at : at + params] = source.astype(jnp.float32).T.astype(jnp.bfloat16)

    all_partner = []
    for t in range(ITERS):
        own, ext, sent_v, sent_p, got_v, got_p = per[t]
        copies_v, copies_p = partner_copies
        all_partner += copies_v + copies_p
        up, down = halo_copies(t)
        ext[pl.ds(HALO, knots)] = own[...]

        @pl.when(has_prev)
        def _():
            up.wait_recv()

        @pl.when(jnp.logical_not(has_prev))
        def _():
            ext[pl.ds(0, HALO)] = jnp.zeros((HALO, params, probes), jnp.bfloat16)

        @pl.when(has_next)
        def _():
            down.wait_recv()

        @pl.when(jnp.logical_not(has_next))
        def _():
            ext[pl.ds(HALO + knots, HALO)] = jnp.zeros((HALO, params, probes), jnp.bfloat16)

        for k in range(knots):
            near = ext[pl.ds(k, 2 * HALO + 1)].reshape((2 * HALO + 1) * params, probes)
            resid[k] = resid[k] - jnp.dot(wide[k], near, preferred_element_type=jnp.float32)

        def scatter(entries, targets):
            for k in range(knots):
                total = resid[k]
                for entry, target in zip(entries, targets):
                    total = total - jnp.where(target == k, entry, 0.0)
                resid[k] = total

        for b in range(buckets):
            copies_v[b].wait_recv()
            entries = [
                jnp.dot(
                    cmask[b * slots + s], got_v[b, s], preferred_element_type=jnp.float32
                )
                for s in range(slots)
            ]
            scatter(entries, [own_index(b, s, 0) for s in range(slots)])
        for b in range(buckets):
            copies_p[b].wait_recv()
            scatter(
                [got_p[b, s].astype(jnp.float32) for s in range(slots)],
                [far_index(b, s) for s in range(slots)],
            )
        coeff_next = 1.0 / (2.0 * center / radius - coeff)
        for k in range(knots):
            fresh = (coeff_next * coeff) * direc[k] + (2.0 * coeff_next / radius) * resid[k]
            direc[k] = fresh
            out[k] = out[k] + fresh
            if t + 1 < ITERS:
                per[t + 1][0][k] = fresh.astype(jnp.bfloat16)
        coeff = coeff_next
        if t + 1 < ITERS:
            start_halos(t + 1)
            partner_copies = start_partners(t + 1)

    for copy in meta_copies + all_partner:
        copy.wait_send()

    @pl.when(has_next)
    def _():
        lower_copy.wait_send()
        for t in range(ITERS):
            halo_copies(t)[0].wait_send()

    @pl.when(has_prev)
    def _():
        for t in range(ITERS):
            halo_copies(t)[1].wait_send()


def body(lines, segs, right_side, band_blocks, knot_pairs, pair_counts, cross_blocks):
    rhs = right_side[0]
    band = band_blocks[0]
    pairs = knot_pairs[0, 0]
    buckets, slots = pairs.shape[:2]
    knots, params, probes = rhs.shape
    cross = cross_blocks.reshape(buckets * slots, params, params)
    group = buckets // 2 + 1
    offsets = [b - (group - 1) if b < group - 1 else b - group + 2 for b in range(buckets)]
    words = jnp.concatenate(
        [jnp.clip(pairs, 0, knots - 1).reshape(-1), pair_counts.reshape(-1)]
    )
    meta = jnp.pad(words, (0, 128 - words.shape[0]))[None]
    meta_vec = jnp.broadcast_to(meta, (8, 128))
    half = jnp.bfloat16
    per = [
        pltpu.VMEM((knots, params, probes), half),
        pltpu.VMEM((knots + 2 * HALO, params, probes), half),
        pltpu.VMEM((buckets, slots, params, probes), half),
        pltpu.VMEM((buckets, slots, params, probes), half),
        pltpu.VMEM((buckets, slots, params, probes), half),
        pltpu.VMEM((buckets, slots, params, probes), half),
    ]
    sems = buckets + 1 + ITERS * (2 * buckets + 2)
    vmem = pl.BlockSpec(memory_space=pltpu.VMEM)
    smem = pl.BlockSpec(memory_space=pltpu.SMEM)
    done = pl.pallas_call(
        functools.partial(kernel, lines, segs, offsets, slots),
        out_shape=jax.ShapeDtypeStruct(rhs.shape, jnp.float32),
        in_specs=[smem, vmem, vmem, vmem, vmem],
        out_specs=vmem,
        scratch_shapes=[
            pltpu.VMEM((knots, params, (2 * HALO + 1) * params), half),
            pltpu.VMEM((buckets * slots, params, params), half),
            pltpu.VMEM((buckets * slots, params, params), half),
            pltpu.VMEM((HALO, HALO + 1, params, params), half),
            pltpu.VMEM((buckets, 8, 128), jnp.int32),
            pltpu.SMEM((buckets, 8, 128), jnp.int32),
            pltpu.VMEM(rhs.shape, jnp.float32),
            pltpu.VMEM(rhs.shape, jnp.float32),
            *(per * ITERS),
            pltpu.SemaphoreType.DMA((sems,)),
            pltpu.SemaphoreType.DMA((sems,)),
            pltpu.SemaphoreType.DMA,
        ],
        compiler_params=pltpu.CompilerParams(
            collective_id=0, has_side_effects=True, vmem_limit_bytes=32 * 2**20
        ),
        name="chebyshev",
    )(meta, meta_vec, rhs, band, cross)
    return done[None]


def solution(mesh):
    return jax.shard_map(
        functools.partial(body, mesh.shape["line"], mesh.shape["seg"]),
        mesh=mesh,
        in_specs=(
            P("line", "seg", None, None),
            P("line", "seg", None, None, None),
            P("line", "seg", None, None, None),
            P("line", "seg", None),
            P("line", "seg", None, None, None, None),
        ),
        out_specs=P("line", "seg", None, None),
        check_vma=False,
    )
```

time: 182 us -> 46.3 us (0.25); the launches traced: 179 us -> 46 us
  starting transfers between devices: 74.3 us -> 0 us
  local copies, waits for them, and re-layouts: 53.9 us -> 5.28 us
  Pallas kernels: 0 us -> 40.7 us
  matrix products: 23.7 us -> 0 us
  waiting for transfers between devices: 17.8 us -> 0 us
  other arithmetic: 7.42 us -> 0.08 us
  between operations: 2.32 us -> 0.02 us
    ppermute x49 -> x0, starting transfers between devices: 74.3 us -> none  [the longest x42 52.7 us: passed_along_2(): return lax.ppermute(x, axis, [(i, (i + by) % count) for i in range(count)])]
    pallas_call x0 -> x1, Pallas kernels: none -> 40.7 us  [body(): pl.pallas_call(functools.partial(kernel, lines, segs, offsets, slots), ou...]
    dot_general x60 -> x0, matrix products: 23.7 us -> none  [the longest x12 9.07 us: body(): jnp.einsum('kab,kbr->kar', blocks[:, step], extended[3 + step:3 + step +...]
    gather x36 -> x0, local copies, waits for them, and re-layouts: 22.5 us -> none  [the longest x18 11.6 us: body(): answer_rows = jnp.take(probe_bf, asked_knots[apply_bucket], axis=0)]
    ppermute x49 -> x0, waiting for transfers between devices: 17.8 us -> none  [the longest x42 17.8 us: passed_along_2(): return lax.ppermute(x, axis, [(i, (i + by) % count) for i in range(count)])]
    concatenate x4 -> x0, local copies, waits for them, and re-layouts: 10.3 us -> none  [the longest x3 10.2 us: body(): target_values = jnp.concatenate(entry_values, axis=0)]
    dot_general x18 -> x0, local copies, waits for them, and re-layouts: 8.35 us -> none  [body(): jnp.einsum('dqp,dpc->dqc', pair_coupling_term[apply_bucket], fetched_rows...]
    slice x6 -> x0, local copies, waits for them, and re-layouts: 5.99 us -> none  [the longest x3 2.01 us: padded(): lax.slice_in_dim(block, 0, width, axis=dim)]
  transfers between devices with their start and end apart: 49 -> 0, of which waited for: 13 -> 0; matrix products, arithmetic and copies ran while one was open for 27% -> 0% of each run, Pallas kernels for 0% -> 0%
where the time goes in v1:
time: 46.3 us; the launch traced here: 46 us
  Pallas kernels  40.7 us (88%)
  local copies, waits for them, and re-layouts  5.28 us (11%)
    pallas_call x1, Pallas kernels, body(): pl.pallas_call(functools.partial(kernel, lines, segs, offsets, slots), ou...  40.7 us
    unnamed x11, local copies, waits for them, and re-layouts  5.08 us

profile of v1, /device:TPU:1, one launch (start us, length us, event | category | flops | bytes accessed | tf_op | source)
XLA Modules:
  0.0 46.0 jit_solution(407929034754751610)
XLA Ops:
  0.0 0.0 copy-start.3
  0.0 0.7 %copy-done.3 = s32[1,1,6,2,2]{2,4,3,1,0:T(2,128)S(1)} copy-done((s32[1,1,6,2,2]{2,4,3,1,0:T(2,128)S(1)}, s32[1,1,6,2,2]{2,4,3,1,0:T(2,128)}, u32[]{:S(2)}) %copy-start.3) | copy-done | bytes 120
  0.7 0.1 copy.7
  0.8 0.0 copy-start.4
  0.8 0.1 min.12
  0.9 0.6 %copy-done.4 = s32[1,1,6]{2,1,0:T(1,128)S(1)} copy-done((s32[1,1,6]{2,1,0:T(1,128)S(1)}, s32[1,1,6]{2,1,0:T(1,128)}, u32[]{:S(2)}) %copy-start.4) | copy-done | bytes 48
  1.4 0.1 pad_add_fusion
  1.5 0.0 copy-start
  1.5 1.1 %copy-done = bf16[1,8,4,96,96]{4,3,2,1,0:T(8,128)(2,1)S(1)} copy-done((bf16[1,8,4,96,96]{4,3,2,1,0:T(8,128)(2,1)S(1)}, bf16[1,8,4,96,96]{4,3,2,1,0:T(8,128)(2,1)}, u32[]{:S(2)}) %copy-start) | copy-done | bytes 589848
  2.7 0.0 copy-start.1
  2.7 1.0 %copy-done.1 = f32[1,8,96,128]{3,2,1,0:T(8,128)S(1)} copy-done((f32[1,8,96,128]{3,2,1,0:T(8,128)S(1)}, f32[1,8,96,128]{3,2,1,0:T(8,128)}, u32[]{:S(2)}) %copy-start.1) | copy-done | bytes 393240
  3.7 0.0 copy-start.2
  3.7 1.0 %copy-done.2 = bf16[1,1,6,2,96,96]{5,4,3,2,1,0:T(8,128)(2,1)S(1)} copy-done((bf16[1,1,6,2,96,96]{5,4,3,2,1,0:T(8,128)(2,1)S(1)}, bf16[1,1,6,2,96,96]{5,4,3,2,1,0:T(8,128)(2,1)}, u32[]{:S(2)}) %copy-start.2) | copy-done | bytes 221208
  4.6 40.7 %chebyshev.1 = f32[8,96,128]{2,1,0:T(8,128)S(1)} custom-call(s32[1,128]{1,0:T(1,128)S(1)} %get-tuple-element.6.refs_0_, s32[8,128]{1,0:T(8,128)S(1)} %broadcast_in_dim.12.refs_1_, f32[8,96,128]{2,1,0:T(8,128)S(1)} %bitcast.9, bf16[8,4,96,96]{3,2,1,0:T(8,128)(2,1)S(1)} %bitcast.8, bf16[12,96,96]{2,1,0:T(8,128)(2,1)S(1)} %bitcast.10), custom_call_target="tpu_custom_call" | custom-call | tf_op jit(solution)/shard_map/chebyshev/pallas_call | solution.py:268
  45.3 0.7 %copy.9 = f32[1,8,96,128]{3,2,1,0:T(8,128)} copy(f32[1,8,96,128]{3,2,1,0:T(8,128)S(1)} %bitcast.7) | data formatting | bytes 786432
  (3 shorter events, 0.0 us)
Async XLA Ops:
  0.0 0.7 %copy-start.3 = (s32[1,1,6,2,2]{2,4,3,1,0:T(2,128)S(1)}, s32[1,1,6,2,2]{2,4,3,1,0:T(2,128)}, u32[]{:S(2)}) copy-start(s32[1,1,6,2,2]{2,4,3,1,0:T(2,128)} %param.7) | copy-start | bytes 292
  0.8 0.7 %copy-start.4 = (s32[1,1,6]{2,1,0:T(1,128)S(1)}, s32[1,1,6]{2,1,0:T(1,128)}, u32[]{:S(2)}) copy-start(s32[1,1,6]{2,1,0:T(1,128)} %param.8) | copy-start | bytes 76
  1.5 1.1 %copy-start = (bf16[1,8,4,96,96]{4,3,2,1,0:T(8,128)(2,1)S(1)}, bf16[1,8,4,96,96]{4,3,2,1,0:T(8,128)(2,1)}, u32[]{:S(2)}) copy-start(bf16[1,8,4,96,96]{4,3,2,1,0:T(8,128)(2,1)} %param.6) | copy-start | bytes 1769476
  2.7 1.0 %copy-start.1 = (f32[1,8,96,128]{3,2,1,0:T(8,128)S(1)}, f32[1,8,96,128]{3,2,1,0:T(8,128)}, u32[]{:S(2)}) copy-start(f32[1,8,96,128]{3,2,1,0:T(8,128)} %param.5) | copy-start | bytes 1179652
  3.7 1.0 %copy-start.2 = (bf16[1,1,6,2,96,96]{5,4,3,2,1,0:T(8,128)(2,1)S(1)}, bf16[1,1,6,2,96,96]{5,4,3,2,1,0:T(8,128)(2,1)}, u32[]{:S(2)}) copy-start(bf16[1,1,6,2,96,96]{5,4,3,2,1,0:T(8,128)(2,1)} %param.9) | copy-start | bytes 663556

commit v2 on v1

v2 whole, which is shorter than its diff:
```python
import functools

import jax
import jax.numpy as jnp
from jax import lax
from jax.experimental import pallas as pl
from jax.experimental.pallas import tpu as pltpu
from jax.sharding import PartitionSpec as P

ITERS = 3
HALO = 3
LO_BOUND = 1.5
HI_BOUND = 12.0
MESH = pl.DeviceIdType.MESH


def kernel(lines, segs, offsets, slots, *refs):
    (count_ref, meta_vec, rhs, band_in, cross_in, out) = refs[:6]
    (wide, band, cross, ctrans, lower, meta_in, meta_far, meta_own, resid, direc) = refs[6:16]
    per = [refs[16 + 6 * t : 22 + 6 * t] for t in range(ITERS)]
    send_sem, recv_sem, local_sem = refs[16 + 6 * ITERS :]
    knots, params, probes = resid.shape
    buckets = len(offsets)
    line = lax.axis_index("line")
    seg = lax.axis_index("seg")
    has_prev = seg > 0
    has_next = seg < segs - 1

    def line_at(shift):
        return (lax.rem(line + (shift + lines), lines), seg)

    prev_dev = (line, jnp.maximum(seg - 1, 0))
    next_dev = (line, jnp.minimum(seg + 1, segs - 1))

    barrier = pltpu.get_barrier_semaphore()
    for off in offsets:
        pl.semaphore_signal(barrier, inc=1, device_id=line_at(off), device_id_type=MESH)

    @pl.when(has_prev)
    def _():
        pl.semaphore_signal(barrier, inc=1, device_id=prev_dev, device_id_type=MESH)

    @pl.when(has_next)
    def _():
        pl.semaphore_signal(barrier, inc=1, device_id=next_dev, device_id_type=MESH)

    load_rhs = pltpu.make_async_copy(rhs, resid, local_sem.at[0])
    load_cross = pltpu.make_async_copy(cross_in, cross, local_sem.at[1])
    load_band = pltpu.make_async_copy(band_in, band, local_sem.at[2])
    load_own = pltpu.make_async_copy(meta_vec, meta_own, local_sem.at[3])
    load_rhs.start()
    load_own.start()
    load_cross.start()
    load_band.start()

    center = (HI_BOUND + LO_BOUND) / 2.0
    radius = (HI_BOUND - LO_BOUND) / 2.0
    coeff = radius / center

    load_rhs.wait()
    for k in range(knots):
        first = resid[k] / center
        direc[k] = first
        out[k] = first
        per[0][0][k] = first.astype(jnp.bfloat16)

    pl.semaphore_wait(
        barrier, buckets + has_prev.astype(jnp.int32) + has_next.astype(jnp.int32)
    )

    def remote(src, dst, sem, device):
        return pltpu.make_async_remote_copy(
            src_ref=src,
            dst_ref=dst,
            send_sem=send_sem.at[sem],
            recv_sem=recv_sem.at[sem],
            device_id=device,
            device_id_type=MESH,
        )

    meta_copies = [
        remote(meta_vec, meta_in.at[b], b, line_at(off)) for b, off in enumerate(offsets)
    ]
    for copy in meta_copies:
        copy.start()
    lower_copy = remote(band_in.at[pl.ds(knots - HALO, HALO)], lower, buckets, next_dev)
    base = buckets + 1
    stride = 2 * buckets + 2

    def halo_copies(t):
        own, ext = per[t][0], per[t][1]
        at = base + t * stride
        up = remote(own.at[pl.ds(knots - HALO, HALO)], ext.at[pl.ds(0, HALO)], at, next_dev)
        down = remote(own.at[pl.ds(0, HALO)], ext.at[pl.ds(HALO + knots, HALO)], at + 1, prev_dev)
        return up, down

    def start_halos(t):
        up, down = halo_copies(t)

        @pl.when(has_next)
        def _():
            up.start()

        @pl.when(has_prev)
        def _():
            down.start()

    def own_index(b, s, which):
        return jnp.clip(meta_own[0, (b * slots + s) * 2 + which], 0, knots - 1)

    def far_index(b, s):
        return jnp.clip(meta_far[b, 0, (b * slots + s) * 2 + 1], 0, knots - 1)

    def asked_copies(t):
        at = base + t * stride + 2
        return [
            remote(per[t][2].at[b], per[t][4].at[b], at + b, line_at(-off))
            for b, off in enumerate(offsets)
        ]

    def product_copies(t):
        at = base + t * stride + 2 + buckets
        return [
            remote(per[t][3].at[b], per[t][5].at[b], at + b, line_at(off))
            for b, off in enumerate(offsets)
        ]

    def start_asked(t):
        for b, copy in enumerate(asked_copies(t)):
            for s in range(slots):
                per[t][2][b, s] = per[t][0][far_index(b, s)]
            copy.start()

    def start_products(t):
        for b, copy in enumerate(product_copies(t)):
            for s in range(slots):
                if t == 0:
                    keep = s < count_ref[b]
                    block = cross[b * slots + s]
                    block = jnp.where(keep, block, jnp.zeros_like(block))
                    cross[b * slots + s] = block
                    ctrans[b * slots + s] = block.T
                per[t][3][b, s] = jnp.dot(
                    ctrans[b * slots + s],
                    per[t][0][own_index(b, s, 0)],
                    preferred_element_type=jnp.float32,
                ).astype(jnp.bfloat16)
            copy.start()

    start_halos(0)

    @pl.when(has_next)
    def _():
        lower_copy.start()

    load_own.wait()
    load_cross.wait()
    start_products(0)
    for copy in meta_copies:
        copy.wait_recv()
    to_scalar = pltpu.make_async_copy(meta_in, meta_far, local_sem.at[4])
    to_scalar.start()
    to_scalar.wait()
    start_asked(0)

    load_band.wait()
    for k in range(knots):
        for step in range(HALO + 1):
            at = (HALO + step) * params
            wide[k, :, at : at + params] = band[k, step]
        for step in range(1, min(k, HALO) + 1):
            at = (HALO - step) * params
            wide[k, :, at : at + params] = band[k - step, step].T

    @pl.when(has_prev)
    def _():
        lower_copy.wait_recv()

    @pl.when(jnp.logical_not(has_prev))
    def _():
        lower[...] = jnp.zeros_like(lower)

    for k in range(HALO):
        for step in range(k + 1, HALO + 1):
            at = (HALO - step) * params
            wide[k, :, at : at + params] = lower[HALO + k - step, step].T

    for t in range(ITERS):
        own, ext, sent_v, sent_p, got_v, got_p = per[t]
        up, down = halo_copies(t)
        ext[pl.ds(HALO, knots)] = own[...]

        @pl.when(has_prev)
        def _():
            up.wait_recv()

        @pl.when(jnp.logical_not(has_prev))
        def _():
            ext[pl.ds(0, HALO)] = jnp.zeros((HALO, params, probes), jnp.bfloat16)

        @pl.when(has_next)
        def _():
            down.wait_recv()

        @pl.when(jnp.logical_not(has_next))
        def _():
            ext[pl.ds(HALO + knots, HALO)] = jnp.zeros((HALO, params, probes), jnp.bfloat16)

        for k in range(knots):
            near = ext[pl.ds(k, 2 * HALO + 1)].reshape((2 * HALO + 1) * params, probes)
            resid[k] = resid[k] - jnp.dot(wide[k], near, preferred_element_type=jnp.float32)

        def scatter(entries, targets):
            for k in range(knots):
                total = resid[k]
                for entry, target in zip(entries, targets):
                    total = total - jnp.where(target == k, entry, 0.0)
                resid[k] = total

        def add_asked():
            for b, copy in enumerate(asked_copies(t)):
                copy.wait_recv()
                entries = [
                    jnp.dot(
                        cross[b * slots + s], got_v[b, s], preferred_element_type=jnp.float32
                    )
                    for s in range(slots)
                ]
                scatter(entries, [own_index(b, s, 0) for s in range(slots)])

        def add_products():
            for b, copy in enumerate(product_copies(t)):
                copy.wait_recv()
                scatter(
                    [got_p[b, s].astype(jnp.float32) for s in range(slots)],
                    [far_index(b, s) for s in range(slots)],
                )

        if t == 0:
            add_products()
            add_asked()
        else:
            add_asked()
            add_products()
        coeff_next = 1.0 / (2.0 * center / radius - coeff)
        for k in range(knots):
            fresh = (coeff_next * coeff) * direc[k] + (2.0 * coeff_next / radius) * resid[k]
            out[k] = out[k] + fresh
            if t + 1 < ITERS:
                direc[k] = fresh
                per[t + 1][0][k] = fresh.astype(jnp.bfloat16)
        coeff = coeff_next
        if t + 1 < ITERS:
            start_halos(t + 1)
            start_asked(t + 1)
            start_products(t + 1)

    for copy in meta_copies:
        copy.wait_send()
    for t in range(ITERS):
        for copy in asked_copies(t) + product_copies(t):
            copy.wait_send()

    @pl.when(has_next)
    def _():
        lower_copy.wait_send()
        for t in range(ITERS):
            halo_copies(t)[0].wait_send()

    @pl.when(has_prev)
    def _():
        for t in range(ITERS):
            halo_copies(t)[1].wait_send()


def body(lines, segs, right_side, band_blocks, knot_pairs, pair_counts, cross_blocks):
    rhs = right_side[0]
    band = band_blocks[0]
    pairs = knot_pairs[0, 0]
    buckets, slots = pairs.shape[:2]
    knots, params, probes = rhs.shape
    cross = cross_blocks.reshape(buckets * slots, params, params)
    group = buckets // 2 + 1
    offsets = [b - (group - 1) if b < group - 1 else b - group + 2 for b in range(buckets)]
    words = pairs.reshape(-1)
    meta = jnp.pad(words, (0, 128 - words.shape[0]))[None]
    half = jnp.bfloat16
    per = [
        pltpu.VMEM((knots, params, probes), half),
        pltpu.VMEM((knots + 2 * HALO, params, probes), half),
        pltpu.VMEM((buckets, slots, params, probes), half),
        pltpu.VMEM((buckets, slots, params, probes), half),
        pltpu.VMEM((buckets, slots, params, probes), half),
        pltpu.VMEM((buckets, slots, params, probes), half),
    ]
    sems = buckets + 1 + ITERS * (2 * buckets + 2)
    vmem = pl.BlockSpec(memory_space=pltpu.VMEM)
    hbm = pl.BlockSpec(memory_space=pltpu.HBM)
    smem = pl.BlockSpec(memory_space=pltpu.SMEM)
    done = pl.pallas_call(
        functools.partial(kernel, lines, segs, offsets, slots),
        out_shape=jax.ShapeDtypeStruct(rhs.shape, jnp.float32),
        in_specs=[smem, vmem, hbm, hbm, hbm],
        out_specs=vmem,
        scratch_shapes=[
            pltpu.VMEM((knots, params, (2 * HALO + 1) * params), half),
            pltpu.VMEM(band.shape, half),
            pltpu.VMEM(cross.shape, half),
            pltpu.VMEM(cross.shape, half),
            pltpu.VMEM((HALO, HALO + 1, params, params), half),
            pltpu.VMEM((buckets, 1, 128), jnp.int32),
            pltpu.SMEM((buckets, 1, 128), jnp.int32),
            pltpu.SMEM((1, 128), jnp.int32),
            pltpu.VMEM(rhs.shape, jnp.float32),
            pltpu.VMEM(rhs.shape, jnp.float32),
            *(per * ITERS),
            pltpu.SemaphoreType.DMA((sems,)),
            pltpu.SemaphoreType.DMA((sems,)),
            pltpu.SemaphoreType.DMA((5,)),
        ],
        compiler_params=pltpu.CompilerParams(
            collective_id=0, has_side_effects=True, vmem_limit_bytes=60 * 2**20
        ),
        name="chebyshev",
    )(pair_counts.reshape(-1), meta, rhs, band, cross)
    return done[None]


def solution(mesh):
    return jax.shard_map(
        functools.partial(body, mesh.shape["line"], mesh.shape["seg"]),
        mesh=mesh,
        in_specs=(
            P("line", "seg", None, None),
            P("line", "seg", None, None, None),
            P("line", "seg", None, None, None),
            P("line", "seg", None),
            P("line", "seg", None, None, None, None),
        ),
        out_specs=P("line", "seg", None, None),
        check_vma=False,
    )
```

time: 46.3 us -> 40.6 us (0.88)
  Pallas kernels: 40.7 us -> 37.2 us
  local copies, waits for them, and re-layouts: 5.28 us -> 3.16 us
    pallas_call x1, Pallas kernels: 40.7 us -> 37.2 us  [body(): pl.pallas_call(functools.partial(kernel, lines, segs, offsets, slots), ou...]
    unnamed x11 -> x4, local copies, waits for them, and re-layouts: 5.08 us -> 2.55 us
    broadcast_in_dim x1, local copies, waits for them, and re-layouts: 0.01 us -> 0.52 us  [body(): meta = jnp.pad(words, (0, 128 - words.shape[0]))[None]]
where the time goes in v2:
time: 40.6 us; the launch traced here: 40.4 us
  Pallas kernels  37.2 us (92%)
  local copies, waits for them, and re-layouts  3.16 us (8%)
    pallas_call x1, Pallas kernels, body(): pl.pallas_call(functools.partial(kernel, lines, segs, offsets, slots), ou...  37.2 us
    unnamed x4, local copies, waits for them, and re-layouts  2.55 us

profile of v2, /device:TPU:1, one launch (start us, length us, event | category | flops | bytes accessed | tf_op | source)
XLA Modules:
  0.0 40.4 jit_solution(18034546725752301367)
XLA Ops:
  0.0 0.0 copy-start
  0.0 0.7 %copy-done = s32[1,1,6,2,2]{2,4,3,1,0:T(2,128)S(1)} copy-done((s32[1,1,6,2,2]{2,4,3,1,0:T(2,128)S(1)}, s32[1,1,6,2,2]{2,4,3,1,0:T(2,128)}, u32[]{:S(2)}) %copy-start) | copy-done | bytes 120
  0.7 0.1 copy.7
  0.8 0.1 reshape_squeeze.3
  0.9 0.5 %pad_bitcast_fusion.refs_1_ = s32[1,128]{1,0:T(1,128)} fusion(s32[24]{0:T(128)S(1)} %reshape_squeeze.3), kind=kLoop, calls=%fused_computation | loop fusion | bytes 608 | tf_op jit(solution)/shard_map/broadcast_in_dim | solution.py:286
  1.4 37.2 %chebyshev.1 = f32[8,96,128]{2,1,0:T(8,128)} custom-call(s32[6]{0:T(128)} %bitcast.11, s32[1,128]{1,0:T(1,128)} %pad_bitcast_fusion.refs_1_, f32[8,96,128]{2,1,0:T(8,128)} %bitcast.9, bf16[8,4,96,96]{3,2,1,0:T(8,128)(2,1)} %bitcast.8, bf16[12,96,96]{2,1,0:T(8,128)(2,1)} %bitcast.10), custom_call_target="tpu_custom_call" | custom-call | tf_op jit(solution)/shard_map/chebyshev/pallas_call | solution.py:300
  38.6 1.8 %copy.9 = f32[1,8,96,128]{3,2,1,0:T(8,128)} copy(f32[1,8,96,128]{3,2,1,0:T(8,128)} %bitcast.7) | data formatting | bytes 786432
Async XLA Ops:
  0.0 0.7 %copy-start = (s32[1,1,6,2,2]{2,4,3,1,0:T(2,128)S(1)}, s32[1,1,6,2,2]{2,4,3,1,0:T(2,128)}, u32[]{:S(2)}) copy-start(s32[1,1,6,2,2]{2,4,3,1,0:T(2,128)} %param.7) | copy-start | bytes 292

commit v3 on v2

--- a/solution.py
+++ b/solution.py
@@ -16,9 +16,9 @@
 
 def kernel(lines, segs, offsets, slots, *refs):
     (count_ref, meta_vec, rhs, band_in, cross_in, out) = refs[:6]
-    (wide, band, cross, ctrans, lower, meta_in, meta_far, meta_own, resid, direc) = refs[6:16]
-    per = [refs[16 + 6 * t : 22 + 6 * t] for t in range(ITERS)]
-    send_sem, recv_sem, local_sem = refs[16 + 6 * ITERS :]
+    (wide, band, cross, ctrans, lower, meta_in, meta_far, meta_own, resid, direc, entry) = refs[6:17]
+    per = [refs[17 + 6 * t : 23 + 6 * t] for t in range(ITERS)]
+    send_sem, recv_sem, local_sem = refs[17 + 6 * ITERS :]
     knots, params, probes = resid.shape
     buckets = len(offsets)
     line = lax.axis_index("line")
@@ -106,10 +106,10 @@
             down.start()
 
     def own_index(b, s, which):
-        return jnp.clip(meta_own[0, (b * slots + s) * 2 + which], 0, knots - 1)
+        return jnp.clip(meta_own[s, which, b], 0, knots - 1)
 
     def far_index(b, s):
-        return jnp.clip(meta_far[b, 0, (b * slots + s) * 2 + 1], 0, knots - 1)
+        return jnp.clip(meta_far[b, s, 1, b], 0, knots - 1)
 
     def asked_copies(t):
         at = base + t * stride + 2
@@ -210,31 +210,29 @@
             near = ext[pl.ds(k, 2 * HALO + 1)].reshape((2 * HALO + 1) * params, probes)
             resid[k] = resid[k] - jnp.dot(wide[k], near, preferred_element_type=jnp.float32)
 
-        def scatter(entries, targets):
+        def scatter(targets):
             for k in range(knots):
                 total = resid[k]
-                for entry, target in zip(entries, targets):
-                    total = total - jnp.where(target == k, entry, 0.0)
+                for e, target in enumerate(targets):
+                    total = total - jnp.where(target == k, entry[e], 0.0)
                 resid[k] = total
 
         def add_asked():
-            for b, copy in enumerate(asked_copies(t)):
+            for copy in asked_copies(t):
                 copy.wait_recv()
-                entries = [
-                    jnp.dot(
-                        cross[b * slots + s], got_v[b, s], preferred_element_type=jnp.float32
-                    )
-                    for s in range(slots)
-                ]
-                scatter(entries, [own_index(b, s, 0) for s in range(slots)])
+            for b in range(buckets):
+                for s in range(slots):
+                    e = b * slots + s
+                    entry[e] = jnp.dot(cross[e], got_v[b, s], preferred_element_type=jnp.float32)
+            scatter([own_index(b, s, 0) for b in range(buckets) for s in range(slots)])
 
         def add_products():
-            for b, copy in enumerate(product_copies(t)):
+            for copy in product_copies(t):
                 copy.wait_recv()
-                scatter(
-                    [got_p[b, s].astype(jnp.float32) for s in range(slots)],
-                    [far_index(b, s) for s in range(slots)],
-                )
+            for b in range(buckets):
+                for s in range(slots):
+                    entry[b * slots + s] = got_p[b, s].astype(jnp.float32)
+            scatter([far_index(b, s) for b in range(buckets) for s in range(slots)])
 
         if t == 0:
             add_products()
@@ -282,8 +280,7 @@
     cross = cross_blocks.reshape(buckets * slots, params, params)
     group = buckets // 2 + 1
     offsets = [b - (group - 1) if b < group - 1 else b - group + 2 for b in range(buckets)]
-    words = pairs.reshape(-1)
-    meta = jnp.pad(words, (0, 128 - words.shape[0]))[None]
+    meta = jnp.transpose(pairs, (1, 2, 0))
     half = jnp.bfloat16
     per = [
         pltpu.VMEM((knots, params, probes), half),
@@ -300,7 +297,7 @@
     done = pl.pallas_call(
         functools.partial(kernel, lines, segs, offsets, slots),
         out_shape=jax.ShapeDtypeStruct(rhs.shape, jnp.float32),
-        in_specs=[smem, vmem, hbm, hbm, hbm],
+        in_specs=[smem, hbm, hbm, hbm, hbm],
         out_specs=vmem,
         scratch_shapes=[
             pltpu.VMEM((knots, params, (2 * HALO + 1) * params), half),
@@ -308,11 +305,12 @@
             pltpu.VMEM(cross.shape, half),
             pltpu.VMEM(cross.shape, half),
             pltpu.VMEM((HALO, HALO + 1, params, params), half),
-            pltpu.VMEM((buckets, 1, 128), jnp.int32),
-            pltpu.SMEM((buckets, 1, 128), jnp.int32),
-            pltpu.SMEM((1, 128), jnp.int32),
+            pltpu.VMEM((buckets, *meta.shape), jnp.int32),
+            pltpu.SMEM((buckets, *meta.shape), jnp.int32),
+            pltpu.SMEM(meta.shape, jnp.int32),
             pltpu.VMEM(rhs.shape, jnp.float32),
             pltpu.VMEM(rhs.shape, jnp.float32),
+            pltpu.VMEM((buckets * slots, params, probes), jnp.float32),
             *(per * ITERS),
             pltpu.SemaphoreType.DMA((sems,)),
             pltpu.SemaphoreType.DMA((sems,)),

time: 40.6 us -> 40 us (0.985)
  local copies, waits for them, and re-layouts: 3.16 us -> 1.77 us
  Pallas kernels: 37.2 us -> 38.1 us
    pallas_call x1, Pallas kernels: 37.2 us -> 38.1 us  [body(): pl.pallas_call(functools.partial(kernel, lines, segs, offsets, slots), ou...]
    unnamed x4 -> x1, local copies, waits for them, and re-layouts: 2.55 us -> 1.77 us
    broadcast_in_dim x1 -> x0, local copies, waits for them, and re-layouts: 0.52 us -> none  [body(): meta = jnp.pad(words, (0, 128 - words.shape[0]))[None]]
where the time goes in v3:
time: 40 us; the launch traced here: 39.8 us
  Pallas kernels  38.1 us (95%)
  local copies, waits for them, and re-layouts  1.77 us (4%)
    pallas_call x1, Pallas kernels, body(): pl.pallas_call(functools.partial(kernel, lines, segs, offsets, slots), ou...  38.1 us
    unnamed x1, local copies, waits for them, and re-layouts  1.77 us

profile of v3, /device:TPU:1, one launch (start us, length us, event | category | flops | bytes accessed | tf_op | source)
XLA Modules:
  0.0 39.8 jit_solution(5957101166735947302)
XLA Ops:
  0.0 38.1 %chebyshev.1 = f32[8,96,128]{2,1,0:T(8,128)} custom-call(s32[6]{0:T(128)} %bitcast.13, s32[2,2,6]{2,1,0:T(2,128)} %bitcast.12, f32[8,96,128]{2,1,0:T(8,128)} %bitcast.10, bf16[8,4,96,96]{3,2,1,0:T(8,128)(2,1)} %bitcast.9, bf16[12,96,96]{2,1,0:T(8,128)(2,1)} %bitcast.11), custom_call_target="tpu_custom_call" | custom-call | tf_op jit(solution)/shard_map/chebyshev/pallas_call | solution.py:297
  38.1 1.8 %copy.7 = f32[1,8,96,128]{3,2,1,0:T(8,128)} copy(f32[1,8,96,128]{3,2,1,0:T(8,128)} %bitcast.8) | data formatting | bytes 786432

commit v4 on v3

--- a/solution.py
+++ b/solution.py
@@ -210,43 +210,45 @@
             near = ext[pl.ds(k, 2 * HALO + 1)].reshape((2 * HALO + 1) * params, probes)
             resid[k] = resid[k] - jnp.dot(wide[k], near, preferred_element_type=jnp.float32)
 
-        def scatter(targets):
+        coeff_next = 1.0 / (2.0 * center / radius - coeff)
+
+        def scatter(targets, last):
             for k in range(knots):
                 total = resid[k]
                 for e, target in enumerate(targets):
                     total = total - jnp.where(target == k, entry[e], 0.0)
-                resid[k] = total
-
-        def add_asked():
+                if not last or t + 1 < ITERS:
+                    resid[k] = total
+                if last:
+                    fresh = (coeff_next * coeff) * direc[k] + (2.0 * coeff_next / radius) * total
+                    out[k] = out[k] + fresh
+                    if t + 1 < ITERS:
+                        direc[k] = fresh
+                        per[t + 1][0][k] = fresh.astype(jnp.bfloat16)
+
+        def add_asked(last):
             for copy in asked_copies(t):
                 copy.wait_recv()
             for b in range(buckets):
                 for s in range(slots):
                     e = b * slots + s
                     entry[e] = jnp.dot(cross[e], got_v[b, s], preferred_element_type=jnp.float32)
-            scatter([own_index(b, s, 0) for b in range(buckets) for s in range(slots)])
-
-        def add_products():
+            scatter([own_index(b, s, 0) for b in range(buckets) for s in range(slots)], last)
+
+        def add_products(last):
             for copy in product_copies(t):
                 copy.wait_recv()
             for b in range(buckets):
                 for s in range(slots):
                     entry[b * slots + s] = got_p[b, s].astype(jnp.float32)
-            scatter([far_index(b, s) for b in range(buckets) for s in range(slots)])
+            scatter([far_index(b, s) for b in range(buckets) for s in range(slots)], last)
 
         if t == 0:
-            add_products()
-            add_asked()
+            add_products(False)
+            add_asked(True)
         else:
-            add_asked()
-            add_products()
-        coeff_next = 1.0 / (2.0 * center / radius - coeff)
-        for k in range(knots):
-            fresh = (coeff_next * coeff) * direc[k] + (2.0 * coeff_next / radius) * resid[k]
-            out[k] = out[k] + fresh
-            if t + 1 < ITERS:
-                direc[k] = fresh
-                per[t + 1][0][k] = fresh.astype(jnp.bfloat16)
+            add_asked(False)
+            add_products(True)
         coeff = coeff_next
         if t + 1 < ITERS:
             start_halos(t + 1)
@@ -296,7 +298,7 @@
     smem = pl.BlockSpec(memory_space=pltpu.SMEM)
     done = pl.pallas_call(
         functools.partial(kernel, lines, segs, offsets, slots),
-        out_shape=jax.ShapeDtypeStruct(rhs.shape, jnp.float32),
+        out_shape=pltpu.VMEM(rhs.shape, jnp.float32),
         in_specs=[smem, hbm, hbm, hbm, hbm],
         out_specs=vmem,
         scratch_shapes=[
@@ -317,7 +319,7 @@
             pltpu.SemaphoreType.DMA((5,)),
         ],
         compiler_params=pltpu.CompilerParams(
-            collective_id=0, has_side_effects=True, vmem_limit_bytes=60 * 2**20
+            collective_id=0, has_side_effects=True, vmem_limit_bytes=56 * 2**20
         ),
         name="chebyshev",
     )(pair_counts.reshape(-1), meta, rhs, band, cross)

time: 40 us -> 38 us (0.950)
  local copies, waits for them, and re-layouts: 1.77 us -> 0.75 us
  Pallas kernels: 38.1 us -> 37.1 us
    unnamed x1, local copies, waits for them, and re-layouts: 1.77 us -> 0.75 us
    pallas_call x1, Pallas kernels: 38.1 us -> 37.1 us  [body(): pl.pallas_call(functools.partial(kernel, lines, segs, offsets, slots), ou...]
where the time goes in v4:
time: 38 us; the launch traced here: 37.8 us
  Pallas kernels  37.1 us (98%)
  local copies, waits for them, and re-layouts  0.75 us (2%)
    pallas_call x1, Pallas kernels, body(): pl.pallas_call(functools.partial(kernel, lines, segs, offsets, slots), ou...  37.1 us

profile of v4, /device:TPU:1, one launch (start us, length us, event | category | flops | bytes accessed | tf_op | source)
XLA Modules:
  0.0 37.8 jit_solution(12627774892641833201)
XLA Ops:
  0.0 37.1 %chebyshev.1 = f32[8,96,128]{2,1,0:T(8,128)S(1)} custom-call(s32[6]{0:T(128)} %bitcast.13, s32[2,2,6]{2,1,0:T(2,128)} %bitcast.12, f32[8,96,128]{2,1,0:T(8,128)} %bitcast.10, bf16[8,4,96,96]{3,2,1,0:T(8,128)(2,1)} %bitcast.9, bf16[12,96,96]{2,1,0:T(8,128)(2,1)} %bitcast.11), custom_call_target="tpu_custom_call" | custom-call | tf_op jit(solution)/shard_map/chebyshev/pallas_call | solution.py:299
  37.1 0.7 %copy.7 = f32[1,8,96,128]{3,2,1,0:T(8,128)} copy(f32[1,8,96,128]{3,2,1,0:T(8,128)S(1)} %bitcast.8) | data formatting | bytes 786432

commit v5 on v3

--- a/solution.py
+++ b/solution.py
@@ -17,8 +17,8 @@
 def kernel(lines, segs, offsets, slots, *refs):
     (count_ref, meta_vec, rhs, band_in, cross_in, out) = refs[:6]
     (wide, band, cross, ctrans, lower, meta_in, meta_far, meta_own, resid, direc, entry) = refs[6:17]
-    per = [refs[17 + 6 * t : 23 + 6 * t] for t in range(ITERS)]
-    send_sem, recv_sem, local_sem = refs[17 + 6 * ITERS :]
+    per = [refs[17 + 7 * t : 24 + 7 * t] for t in range(ITERS)]
+    send_sem, recv_sem, local_sem = refs[17 + 7 * ITERS :]
     knots, params, probes = resid.shape
     buckets = len(offsets)
     line = lax.axis_index("line")
@@ -62,7 +62,7 @@
         first = resid[k] / center
         direc[k] = first
         out[k] = first
-        per[0][0][k] = first.astype(jnp.bfloat16)
+        per[0][6][k] = first.astype(jnp.bfloat16)
 
     pl.semaphore_wait(
         barrier, buckets + has_prev.astype(jnp.int32) + has_next.astype(jnp.int32)
@@ -85,10 +85,13 @@
         copy.start()
     lower_copy = remote(band_in.at[pl.ds(knots - HALO, HALO)], lower, buckets, next_dev)
     base = buckets + 1
-    stride = 2 * buckets + 2
+    stride = 4 * buckets + 2
+    lane = lax.broadcasted_iota(jnp.int32, (params, probes), 1)
+    split = probes // 2
+    sides = [lane < split, lane >= split]
 
     def halo_copies(t):
-        own, ext = per[t][0], per[t][1]
+        own, ext = per[t][6], per[t][1]
         at = base + t * stride
         up = remote(own.at[pl.ds(knots - HALO, HALO)], ext.at[pl.ds(0, HALO)], at, next_dev)
         down = remote(own.at[pl.ds(0, HALO)], ext.at[pl.ds(HALO + knots, HALO)], at + 1, prev_dev)
@@ -111,40 +114,60 @@
     def far_index(b, s):
         return jnp.clip(meta_far[b, s, 1, b], 0, knots - 1)
 
-    def asked_copies(t):
-        at = base + t * stride + 2
+    def asked_copies(t, h):
+        at = base + t * stride + 2 + 2 * h * buckets
         return [
-            remote(per[t][2].at[b], per[t][4].at[b], at + b, line_at(-off))
+            remote(per[t][2].at[h, b], per[t][4].at[h, b], at + b, line_at(-off))
             for b, off in enumerate(offsets)
         ]
 
-    def product_copies(t):
-        at = base + t * stride + 2 + buckets
+    def product_copies(t, h):
+        at = base + t * stride + 2 + (2 * h + 1) * buckets
         return [
-            remote(per[t][3].at[b], per[t][5].at[b], at + b, line_at(off))
+            remote(per[t][3].at[h, b], per[t][5].at[h, b], at + b, line_at(off))
             for b, off in enumerate(offsets)
         ]
 
-    def start_asked(t):
-        for b, copy in enumerate(asked_copies(t)):
+    def source(t, h):
+        return per[t][0 if h == 0 and t > 0 else 6]
+
+    def packed(h, blocks):
+        first, second = blocks
+        if h == 0:
+            second = pltpu.roll(second, split, 1)
+        else:
+            first = pltpu.roll(first, split, 1)
+        return jnp.where(sides[0], first, second).astype(jnp.bfloat16)
+
+    def unpacked(h, s, block):
+        if s != h:
+            block = pltpu.roll(block, split, 1)
+        return jnp.where(sides[h], block, 0.0)
+
+    def start_asked(t, h):
+        for b, copy in enumerate(asked_copies(t, h)):
+            blocks = [source(t, h)[far_index(b, s)].astype(jnp.float32) for s in range(slots)]
+            per[t][2][h, b] = packed(h, blocks)
+            copy.start()
+
+    def start_products(t, h):
+        for b, copy in enumerate(product_copies(t, h)):
+            blocks = []
             for s in range(slots):
-                per[t][2][b, s] = per[t][0][far_index(b, s)]
-            copy.start()
-
-    def start_products(t):
-        for b, copy in enumerate(product_copies(t)):
-            for s in range(slots):
-                if t == 0:
+                if t == 0 and h == 0:
                     keep = s < count_ref[b]
                     block = cross[b * slots + s]
                     block = jnp.where(keep, block, jnp.zeros_like(block))
                     cross[b * slots + s] = block
                     ctrans[b * slots + s] = block.T
-                per[t][3][b, s] = jnp.dot(
-                    ctrans[b * slots + s],
-                    per[t][0][own_index(b, s, 0)],
-                    preferred_element_type=jnp.float32,
-                ).astype(jnp.bfloat16)
+                blocks.append(
+                    jnp.dot(
+                        ctrans[b * slots + s],
+                        source(t, h)[own_index(b, s, 0)],
+                        preferred_element_type=jnp.float32,
+                    )
+                )
+            per[t][3][h, b] = packed(h, blocks)
             copy.start()
 
     start_halos(0)
@@ -155,13 +178,15 @@
 
     load_own.wait()
     load_cross.wait()
-    start_products(0)
+    start_products(0, 0)
     for copy in meta_copies:
         copy.wait_recv()
     to_scalar = pltpu.make_async_copy(meta_in, meta_far, local_sem.at[4])
     to_scalar.start()
     to_scalar.wait()
-    start_asked(0)
+    start_asked(0, 0)
+    start_products(0, 1)
+    start_asked(0, 1)
 
     load_band.wait()
     for k in range(knots):
@@ -186,7 +211,7 @@
             wide[k, :, at : at + params] = lower[HALO + k - step, step].T
 
     for t in range(ITERS):
-        own, ext, sent_v, sent_p, got_v, got_p = per[t]
+        _, ext, _, _, got_v, got_p, own = per[t]
         up, down = halo_copies(t)
         ext[pl.ds(HALO, knots)] = own[...]
 
@@ -209,6 +234,10 @@
         for k in range(knots):
             near = ext[pl.ds(k, 2 * HALO + 1)].reshape((2 * HALO + 1) * params, probes)
             resid[k] = resid[k] - jnp.dot(wide[k], near, preferred_element_type=jnp.float32)
+
+        coeff_next = 1.0 / (2.0 * center / radius - coeff)
+
+        coeff_next = 1.0 / (2.0 * center / radius - coeff)
 
         def scatter(targets):
             for k in range(knots):
@@ -217,47 +246,52 @@
                     total = total - jnp.where(target == k, entry[e], 0.0)
                 resid[k] = total
 
-        def add_asked():
-            for copy in asked_copies(t):
+        def add_asked(h):
+            for copy in asked_copies(t, h):
                 copy.wait_recv()
             for b in range(buckets):
                 for s in range(slots):
                     e = b * slots + s
-                    entry[e] = jnp.dot(cross[e], got_v[b, s], preferred_element_type=jnp.float32)
+                    term = jnp.dot(cross[e], got_v[h, b], preferred_element_type=jnp.float32)
+                    entry[e] = unpacked(h, s, term)
             scatter([own_index(b, s, 0) for b in range(buckets) for s in range(slots)])
 
-        def add_products():
-            for copy in product_copies(t):
+        def add_products(h):
+            for copy in product_copies(t, h):
                 copy.wait_recv()
             for b in range(buckets):
                 for s in range(slots):
-                    entry[b * slots + s] = got_p[b, s].astype(jnp.float32)
+                    entry[b * slots + s] = unpacked(h, s, got_p[h, b].astype(jnp.float32))
             scatter([far_index(b, s) for b in range(buckets) for s in range(slots)])
 
-        if t == 0:
-            add_products()
-            add_asked()
-        else:
-            add_asked()
-            add_products()
-        coeff_next = 1.0 / (2.0 * center / radius - coeff)
-        for k in range(knots):
-            fresh = (coeff_next * coeff) * direc[k] + (2.0 * coeff_next / radius) * resid[k]
-            out[k] = out[k] + fresh
+        for h in range(2):
+            if t == 0:
+                add_products(h)
+                add_asked(h)
+            else:
+                add_asked(h)
+                add_products(h)
+            for k in range(knots):
+                old = direc[k]
+                fresh = (coeff_next * coeff) * old + (2.0 * coeff_next / radius) * resid[k]
+                out[k] = out[k] + jnp.where(sides[h], fresh, 0.0)
+                if t + 1 < ITERS:
+                    fresh = jnp.where(sides[h], fresh, old)
+                    direc[k] = fresh
+                    per[t + 1][0 if h == 0 else 6][k] = fresh.astype(jnp.bfloat16)
             if t + 1 < ITERS:
-                direc[k] = fresh
-                per[t + 1][0][k] = fresh.astype(jnp.bfloat16)
+                if h == 1:
+                    start_halos(t + 1)
+                start_asked(t + 1, h)
+                start_products(t + 1, h)
         coeff = coeff_next
-        if t + 1 < ITERS:
-            start_halos(t + 1)
-            start_asked(t + 1)
-            start_products(t + 1)
 
     for copy in meta_copies:
         copy.wait_send()
     for t in range(ITERS):
-        for copy in asked_copies(t) + product_copies(t):
-            copy.wait_send()
+        for h in range(2):
+            for copy in asked_copies(t, h) + product_copies(t, h):
+                copy.wait_send()
 
     @pl.when(has_next)
     def _():
@@ -285,18 +319,16 @@
     per = [
         pltpu.VMEM((knots, params, probes), half),
         pltpu.VMEM((knots + 2 * HALO, params, probes), half),
-        pltpu.VMEM((buckets, slots, params, probes), half),
-        pltpu.VMEM((buckets, slots, params, probes), half),
-        pltpu.VMEM((buckets, slots, params, probes), half),
-        pltpu.VMEM((buckets, slots, params, probes), half),
+        *([pltpu.VMEM((2, buckets, params, probes), half)] * 4),
+        pltpu.VMEM((knots, params, probes), half),
     ]
-    sems = buckets + 1 + ITERS * (2 * buckets + 2)
+    sems = buckets + 1 + ITERS * (4 * buckets + 2)
     vmem = pl.BlockSpec(memory_space=pltpu.VMEM)
     hbm = pl.BlockSpec(memory_space=pltpu.HBM)
     smem = pl.BlockSpec(memory_space=pltpu.SMEM)
     done = pl.pallas_call(
         functools.partial(kernel, lines, segs, offsets, slots),
-        out_shape=jax.ShapeDtypeStruct(rhs.shape, jnp.float32),
+        out_shape=pltpu.VMEM(rhs.shape, jnp.float32),
         in_specs=[smem, hbm, hbm, hbm, hbm],
         out_specs=vmem,
         scratch_shapes=[
@@ -317,7 +349,7 @@
             pltpu.SemaphoreType.DMA((5,)),
         ],
         compiler_params=pltpu.CompilerParams(
-            collective_id=0, has_side_effects=True, vmem_limit_bytes=60 * 2**20
+            collective_id=0, has_side_effects=True, vmem_limit_bytes=56 * 2**20
         ),
         name="chebyshev",
     )(pair_counts.reshape(-1), meta, rhs, band, cross)

time: 40 us -> 37.4 us (0.935)
  Pallas kernels: 38.1 us -> 36.2 us
  local copies, waits for them, and re-layouts: 1.77 us -> 0.75 us
    pallas_call x1, Pallas kernels: 38.1 us -> 36.2 us  [body(): pl.pallas_call(functools.partial(kernel, lines, segs, offsets, slots), ou...]
    unnamed x1, local copies, waits for them, and re-layouts: 1.77 us -> 0.75 us
where the time goes in v5:
time: 37.4 us; the launch traced here: 36.9 us
  Pallas kernels  36.2 us (97%)
  local copies, waits for them, and re-layouts  0.75 us (2%)
    pallas_call x1, Pallas kernels, body(): pl.pallas_call(functools.partial(kernel, lines, segs, offsets, slots), ou...  36.2 us
    unnamed x1, local copies, waits for them, and re-layouts  0.75 us

profile of v5, /device:TPU:1, one launch (start us, length us, event | category | flops | bytes accessed | tf_op | source)
XLA Modules:
  0.0 36.9 jit_solution(15467271533044508015)
XLA Ops:
  0.0 36.2 %chebyshev.1 = f32[8,96,128]{2,1,0:T(8,128)S(1)} custom-call(s32[6]{0:T(128)} %bitcast.13, s32[2,2,6]{2,1,0:T(2,128)} %bitcast.12, f32[8,96,128]{2,1,0:T(8,128)} %bitcast.10, bf16[8,4,96,96]{3,2,1,0:T(8,128)(2,1)} %bitcast.9, bf16[12,96,96]{2,1,0:T(8,128)(2,1)} %bitcast.11), custom_call_target="tpu_custom_call" | custom-call | tf_op jit(solution)/shard_map/chebyshev/pallas_call | solution.py:329
  36.2 0.7 %copy.7 = f32[1,8,96,128]{3,2,1,0:T(8,128)} copy(f32[1,8,96,128]{3,2,1,0:T(8,128)S(1)} %bitcast.8) | data formatting | bytes 786432

commit v6 on v5

--- a/solution.py
+++ b/solution.py
@@ -21,6 +21,7 @@
     send_sem, recv_sem, local_sem = refs[17 + 7 * ITERS :]
     knots, params, probes = resid.shape
     buckets = len(offsets)
+    order = sorted(range(buckets), key=lambda b: (abs(offsets[b]) == 1, abs(offsets[b]), b))
     line = lax.axis_index("line")
     seg = lax.axis_index("seg")
     has_prev = seg > 0
@@ -83,8 +84,16 @@
     ]
     for copy in meta_copies:
         copy.start()
-    lower_copy = remote(band_in.at[pl.ds(knots - HALO, HALO)], lower, buckets, next_dev)
-    base = buckets + 1
+    lower_copies = [
+        remote(
+            band_in.at[knots - HALO + j, pl.ds(HALO - j, j + 1)],
+            lower.at[j, pl.ds(HALO - j, j + 1)],
+            buckets + j,
+            next_dev,
+        )
+        for j in range(HALO)
+    ]
+    base = buckets + HALO
     stride = 4 * buckets + 2
     lane = lax.broadcasted_iota(jnp.int32, (params, probes), 1)
     split = probes // 2
@@ -145,13 +154,17 @@
         return jnp.where(sides[h], block, 0.0)
 
     def start_asked(t, h):
-        for b, copy in enumerate(asked_copies(t, h)):
+        copies = asked_copies(t, h)
+        for b in order:
+            copy = copies[b]
             blocks = [source(t, h)[far_index(b, s)].astype(jnp.float32) for s in range(slots)]
             per[t][2][h, b] = packed(h, blocks)
             copy.start()
 
     def start_products(t, h):
-        for b, copy in enumerate(product_copies(t, h)):
+        copies = product_copies(t, h)
+        for b in order:
+            copy = copies[b]
             blocks = []
             for s in range(slots):
                 if t == 0 and h == 0:
@@ -174,7 +187,8 @@
 
     @pl.when(has_next)
     def _():
-        lower_copy.start()
+        for copy in lower_copies:
+            copy.start()
 
     load_own.wait()
     load_cross.wait()
@@ -199,7 +213,8 @@
 
     @pl.when(has_prev)
     def _():
-        lower_copy.wait_recv()
+        for copy in lower_copies:
+            copy.wait_recv()
 
     @pl.when(jnp.logical_not(has_prev))
     def _():
@@ -295,7 +310,8 @@
 
     @pl.when(has_next)
     def _():
-        lower_copy.wait_send()
+        for copy in lower_copies:
+            copy.wait_send()
         for t in range(ITERS):
             halo_copies(t)[0].wait_send()
 
@@ -322,7 +338,7 @@
         *([pltpu.VMEM((2, buckets, params, probes), half)] * 4),
         pltpu.VMEM((knots, params, probes), half),
     ]
-    sems = buckets + 1 + ITERS * (4 * buckets + 2)
+    sems = buckets + HALO + ITERS * (4 * buckets + 2)
     vmem = pl.BlockSpec(memory_space=pltpu.VMEM)
     hbm = pl.BlockSpec(memory_space=pltpu.HBM)
     smem = pl.BlockSpec(memory_space=pltpu.SMEM)

time: 37.4 us -> 38.2 us (1.021)
  Pallas kernels: 36.2 us -> 36.9 us
    pallas_call x1, Pallas kernels: 36.2 us -> 36.9 us  [body(): pl.pallas_call(functools.partial(kernel, lines, segs, offsets, slots), ou...]
where the time goes in v6:
time: 38.2 us; the launch traced here: 37.7 us
  Pallas kernels  36.9 us (97%)
  local copies, waits for them, and re-layouts  0.75 us (2%)
    pallas_call x1, Pallas kernels, body(): pl.pallas_call(functools.partial(kernel, lines, segs, offsets, slots), ou...  36.9 us

profile of v6, /device:TPU:1, one launch (start us, length us, event | category | flops | bytes accessed | tf_op | source)
XLA Modules:
  0.0 37.7 jit_solution(4871582967807139964)
XLA Ops:
  0.0 36.9 %chebyshev.1 = f32[8,96,128]{2,1,0:T(8,128)S(1)} custom-call(s32[6]{0:T(128)} %bitcast.13, s32[2,2,6]{2,1,0:T(2,128)} %bitcast.12, f32[8,96,128]{2,1,0:T(8,128)} %bitcast.10, bf16[8,4,96,96]{3,2,1,0:T(8,128)(2,1)} %bitcast.9, bf16[12,96,96]{2,1,0:T(8,128)(2,1)} %bitcast.11), custom_call_target="tpu_custom_call" | custom-call | tf_op jit(solution)/shard_map/chebyshev/pallas_call | solution.py:345
  36.9 0.7 %copy.7 = f32[1,8,96,128]{3,2,1,0:T(8,128)} copy(f32[1,8,96,128]{3,2,1,0:T(8,128)S(1)} %bitcast.8) | data formatting | bytes 786432
